TPU v7x, 128 devices: a whole 4x4x4 slice. The times are simulated.
128 devices in a mesh: seq: 8 (over x, y_hi), res: 16 (over y_lo, z, core).
Axes of the slice: x: 4, y: 4 (y_hi: 2, y_lo: 2; y = y_hi * 2 + y_lo), z: 4, core: 2. Of those that a mesh axis runs over, the one named last changes fastest.
Arguments:
- alignment: bfloat16 [256, 512, 256], P('seq', 'res'), may hold values from -6 to 6
- pair_state: bfloat16 [512, 512, 128], P('seq', 'res'), may hold values from -6 to 6
- bias_weight: bfloat16 [128, 8], replicated, may hold values from -15 to 15
- row_weight: bfloat16 [256, 1024], replicated, may hold values from -0.375 to 0.375
- row_output_weight: bfloat16 [256, 256], replicated, may hold values from -0.375 to 0.375
- column_weight: bfloat16 [256, 1024], replicated, may hold values from -2 to 2
- column_output_weight: bfloat16 [256, 256], replicated, may hold values from -0.375 to 0.375
- transition_in: bfloat16 [256, 1024], replicated, may hold values from -0.375 to 0.375
- transition_out: bfloat16 [1024, 256], replicated, may hold values from -0.1875 to 0.1875
- outer_in: bfloat16 [256, 64], replicated, may hold values from -0.375 to 0.375
- outer_out: bfloat16 [1024, 128], replicated, may hold values from -1 to 1
Outputs:
- alignment_out: bfloat16 [256, 512, 256], P(None, ('seq', 'res'))
- pair_update: bfloat16 [512, 512, 128], P('seq', 'res')
All inputs are finite; a program needn't handle non-finite values.
Results may differ from a plain program's by a relative error of at most 0.02.
The roundings to bfloat16 on the way count: a program that leaves them out, or rounds other values in their place, can miss the bound.
Values may be sent and summed in bfloat16 or wider, within the bound.
A program may use at most 128 MiB of HBM per device.

v0:
```python
import jax
import jax.numpy as jnp
from jax import lax
from jax.sharding import PartitionSpec as P

H = 8


epsilon = 1e-05


def from_root(value, axis, source):
    kept = jnp.where(lax.axis_index(axis) == source, value, 0).astype(value.dtype)
    return lax.psum(kept, axis)


def apply_layer_norm(values):
    values = values.astype(jnp.float32)
    center = values - jnp.mean(values, axis=-1, keepdims=True)
    spread = jnp.mean(center * center, axis=-1, keepdims=True)
    return center / jnp.sqrt(spread + epsilon)


def project_heads(normed_input, weight):
    channels = weight.shape[0]
    head_size = channels // H
    projected = jnp.dot(normed_input, weight, preferred_element_type=jnp.float32)
    queries = (projected[..., :channels] * head_size ** (-0.5)).astype(jnp.bfloat16)
    key_rows = projected[..., channels : 2 * channels].astype(jnp.bfloat16)
    value_rows = projected[..., 2 * channels : 3 * channels].astype(jnp.bfloat16)
    gating = jax.nn.sigmoid(projected[..., 3 * channels :]).astype(jnp.bfloat16)
    return (queries, key_rows, value_rows, gating)


def attend_one(queries, key_rows, value_rows, bias):
    length, channels = queries.shape
    head_size = channels // H
    query_heads = queries.reshape(length, H, head_size)
    key_heads = key_rows.reshape(key_rows.shape[0], H, head_size)
    value_heads = value_rows.reshape(value_rows.shape[0], H, head_size)
    scores = jnp.einsum("qhd,khd->hqk", query_heads, key_heads, preferred_element_type=jnp.float32)
    scores = scores + bias.astype(jnp.float32)
    row_peak = jnp.max(scores, axis=-1, keepdims=True)
    exp_terms = jnp.exp(scores - row_peak)
    weights_bf = (exp_terms / jnp.sum(exp_terms, axis=-1, keepdims=True)).astype(jnp.bfloat16)
    result = jnp.einsum("hqk,khd->qhd", weights_bf, value_heads, preferred_element_type=jnp.float32)
    return result.reshape(length, channels)


def column_attend(queries, key_rows, value_rows):
    seq_count, cells, channels = queries.shape
    head_size = channels // H
    query_heads = queries.reshape(seq_count, cells, H, head_size)
    key_heads = key_rows.reshape(seq_count, cells, H, head_size)
    value_heads = value_rows.reshape(seq_count, cells, H, head_size)
    scores = jnp.einsum(
        "sihd,tihd->ihst", query_heads, key_heads, preferred_element_type=jnp.float32
    )
    row_peak = jnp.max(scores, axis=-1, keepdims=True)
    exp_terms = jnp.exp(scores - row_peak)
    weights_bf = (exp_terms / jnp.sum(exp_terms, axis=-1, keepdims=True)).astype(jnp.bfloat16)
    result = jnp.einsum(
        "ihst,tihd->sihd", weights_bf, value_heads, preferred_element_type=jnp.float32
    )
    return result.reshape(seq_count, cells, channels)


def body(
    alignment,
    pair_state,
    bias_weight,
    row_weight,
    row_output_weight,
    column_weight,
    column_output_weight,
    transition_in,
    transition_out,
    outer_in,
    outer_out,
):
    res_cells = alignment.shape[1]
    alignment_rows_state = lax.all_to_all(alignment, "res", split_axis=0, concat_axis=1, tiled=True)
    normed_input = apply_layer_norm(alignment_rows_state).astype(jnp.bfloat16)
    pair_norm = apply_layer_norm(pair_state).astype(jnp.bfloat16)
    tile_bias = (
        jnp.dot(pair_norm, bias_weight, preferred_element_type=jnp.float32)
        .astype(jnp.bfloat16)
        .transpose(2, 0, 1)
    )
    queries, key_rows, value_rows, gating = project_heads(normed_input, row_weight)
    column_bias = lax.all_gather(tile_bias, "seq", axis=1, tiled=True)
    full_bias = lax.all_gather(column_bias, "res", axis=2, tiled=True)

    def one_sequence(inputs):
        return attend_one(inputs[0], inputs[1], inputs[2], full_bias)

    outputs = lax.map(one_sequence, (queries, key_rows, value_rows))
    gated_output_rows = (gating.astype(jnp.float32) * outputs).astype(jnp.bfloat16)
    row_alignment_state = (
        alignment_rows_state.astype(jnp.float32)
        + jnp.dot(gated_output_rows, row_output_weight, preferred_element_type=jnp.float32)
    ).astype(jnp.bfloat16)
    column_alignment_state = lax.all_to_all(
        row_alignment_state, ("seq", "res"), split_axis=1, concat_axis=0, tiled=True
    )
    column_normed_input = apply_layer_norm(column_alignment_state).astype(jnp.bfloat16)
    col_queries, col_keys, col_values, col_gating = project_heads(
        column_normed_input, column_weight
    )
    col_out = column_attend(col_queries, col_keys, col_values)
    column_gated_result = (col_gating.astype(jnp.float32) * col_out).astype(jnp.bfloat16)
    residual_state = column_alignment_state.astype(jnp.float32) + jnp.dot(
        column_gated_result, column_output_weight, preferred_element_type=jnp.float32
    )
    trans_normed = apply_layer_norm(residual_state).astype(jnp.bfloat16)
    hidden = jax.nn.relu(
        jnp.dot(trans_normed, transition_in, preferred_element_type=jnp.float32)
    ).astype(jnp.bfloat16)
    alignment_out = (
        residual_state + jnp.dot(hidden, transition_out, preferred_element_type=jnp.float32)
    ).astype(jnp.bfloat16)
    opm_normed = apply_layer_norm(alignment_out).astype(jnp.bfloat16)
    factors = jnp.dot(opm_normed, outer_in, preferred_element_type=jnp.float32).astype(jnp.bfloat16)
    row_side = lax.all_gather(factors, "res", axis=1, tiled=True)
    outer_width = factors.shape[2] // 2
    row_ratio = lax.axis_size("res") // lax.axis_size("seq")
    left_rows = row_side[:, :, :outer_width]
    right_block = from_root(row_side[:, :, outer_width:], "seq", lax.axis_index("res") // row_ratio)
    right_cols = lax.dynamic_slice_in_dim(
        right_block, lax.axis_index("res") % row_ratio * res_cells, res_cells, 1
    )
    seq_total = row_side.shape[0]
    blocks = []
    for part_index in range(row_ratio):
        left_block = left_rows[:, part_index * res_cells : (part_index + 1) * res_cells]
        outer_sum = (
            jnp.einsum("sic,sjd->ijcd", left_block, right_cols, preferred_element_type=jnp.float32)
            / seq_total
        )
        flattened = outer_sum.astype(jnp.bfloat16).reshape(
            res_cells, res_cells, outer_width * outer_width
        )
        blocks.append(
            jnp.dot(flattened, outer_out, preferred_element_type=jnp.float32).astype(jnp.bfloat16)
        )
    pair_update = jnp.concatenate(blocks, axis=0)
    return (alignment_out, pair_update)


def solution(mesh):
    in_specs = (
        P("seq", "res", None),
        P("seq", "res", None),
        P(),
        P(),
        P(),
        P(),
        P(),
        P(),
        P(),
        P(),
        P(),
    )
    out_specs = (P(None, ("seq", "res"), None), P("seq", "res", None))
    return jax.shard_map(body, mesh=mesh, in_specs=in_specs, out_specs=out_specs, check_vma=False)
```

profile of v0, /device:TPU:1, one launch (start us, length us, event | category | flops | bytes accessed | tf_op | source)
XLA Modules:
  0.0 357.5 jit_solution(9267975305068646164)
XLA Ops:
  12.3 32.7 %all_gather.9 = bf16[8,512,32]{2,0,1:T(8,128)(2,1)S(1)} all-gather(bf16[8,64,32]{2,0,1:T(8,128)(2,1)S(1)} %fusion.18), channel_id=1, replica_groups=mesh['seq'=8,'res'=16] {'seq'}, dimensions={1}, use_global_device_ids=true | all-gather | bytes 294912 | tf_op jit(solution)/shard_map/all_gather | solution.py:91
  46.7 11.9 %all-to-all-start = ((bf16[32,32,256]{2,1,0:T(8,128)(2,1)}), bf16[32,32,256]{2,1,0:T(8,128)(2,1)S(1)}, u32[]{:S(2)}, u32[]{:S(2)}) async-start(bf16[32,32,256]{2,1,0:T(8,128)(2,1)} %param.13), calls=%async_computation | async-start | bytes 1048576 | tf_op jit(solution)/shard_map/all_to_all | solution.py:82
  58.8 10.7 %all-to-all-done = bf16[32,32,256]{2,1,0:T(8,128)(2,1)S(1)} async-done(((bf16[32,32,256]{2,1,0:T(8,128)(2,1)}), bf16[32,32,256]{2,1,0:T(8,128)(2,1)S(1)}, u32[]{:S(2)}, u32[]{:S(2)}) %all-to-all-start) | async-done | bytes 524320 | tf_op jit(solution)/shard_map/all_to_all | solution.py:82
  73.7 19.7 %all-gather.3.cloned.1.call-done = bf16[8,512,512]{1,0,2:T(8,128)(2,1)} async-done(((bf16[8,512,32]{1,0,2:T(8,128)(2,1)}), bf16[8,512,512]{1,0,2:T(8,128)(2,1)}) %all-gather.3.cloned.1.call-update) | async-done | bytes 4194320 | tf_op jit(solution)/shard_map/all_gather | solution.py:92
  93.5 5.6 %copy.81 = bf16[8,512,512]{1,2,0:T(8,128)(2,1)} copy(bf16[8,512,512]{1,0,2:T(8,128)(2,1)} %all-gather.3.cloned.1.call-done) | data formatting | bytes 8388608 | tf_op jit(solution)/shard_map/while | solution.py:97
  99.0 23.1 %while.10 = (s32[]{:T(128)}, f32[2,512,256]{2,1,0:T(8,128)}, bf16[2,512,256]{2,1,0:T(8,128)(2,1)S(1)}, bf16[2,512,256]{2,1,0:T(8,128)(2,1)S(1)}, bf16[2,512,256]...) while((s32[]{:T(128)}, f32[2,512,256]{2,1,0:T(8,128)}, bf16[2,512,256]{2,1,0:T(8,128)(2,1)S(1)}, ...), condition=%wide.region_7.8_spmd, body=%wide.region_4.7_spmd.sunk | while | flops 421532672 | bytes 15499361 | solution.py:97
  99.5 4.4 %fusion.112 = f32[8,512]{1,0:T(8,128)S(1)} fusion(bf16[8,512,512]{1,2,0:T(8,128)(2,1)} %get-tuple-element.153, bf16[512,8,32]{0,2,1:T(8,128)(2,1)S(1)} %bitcast.141, bf16[512,8,32]{0,2,1:T(8,128)(2,1)S(1)} %bitcast.143), kind=kOutput, calls=%fused_computation.117.clone.1 | convolution fusion | flops 142606848 | bytes 4734976 | tf_op jit(solution)/shard_map/while/body/eval_jaxpr/sub | solution.py:44
  104.0 5.6 %fusion.113 = f32[8,32,512]{2,1,0:T(8,128)S(1)} fusion(bf16[512,8,32]{0,2,1:T(8,128)(2,1)S(1)} %bitcast.140, f32[8,512]{1,0:T(8,128)S(1)} %fusion.112, bf16[8,512,512]{1,2,0:T(8,128)(2,1)} %get-tuple-element.153, bf16[512,8,32]{0,2,1:T(8,128)(2,1)S(1)} %bitcast.142, bf16[512,8,32]{0,2,1:T(8,128)(2,1)S(1)} %bitcast.144), kind=kOutput, calls=%fused_computation.5.clone.1 | convolution fusion | flops 278925824 | bytes 5521408 | tf_op jit(solution)/shard_map/while/body/eval_jaxpr/hqk,khd->qhd/dot_general | solution.py:46
  111.1 4.4 %fusion.112 = f32[8,512]{1,0:T(8,128)S(1)} fusion(bf16[8,512,512]{1,2,0:T(8,128)(2,1)} %get-tuple-element.153, bf16[512,8,32]{0,2,1:T(8,128)(2,1)S(1)} %bitcast.141, bf16[512,8,32]{0,2,1:T(8,128)(2,1)S(1)} %bitcast.143), kind=kOutput, calls=%fused_computation.117.clone.1 | convolution fusion | flops 142606848 | bytes 4734976 | tf_op jit(solution)/shard_map/while/body/eval_jaxpr/sub | solution.py:44
  115.5 5.6 %fusion.113 = f32[8,32,512]{2,1,0:T(8,128)S(1)} fusion(bf16[512,8,32]{0,2,1:T(8,128)(2,1)S(1)} %bitcast.140, f32[8,512]{1,0:T(8,128)S(1)} %fusion.112, bf16[8,512,512]{1,2,0:T(8,128)(2,1)} %get-tuple-element.153, bf16[512,8,32]{0,2,1:T(8,128)(2,1)S(1)} %bitcast.142, bf16[512,8,32]{0,2,1:T(8,128)(2,1)S(1)} %bitcast.144), kind=kOutput, calls=%fused_computation.5.clone.1 | convolution fusion | flops 278925824 | bytes 5521408 | tf_op jit(solution)/shard_map/while/body/eval_jaxpr/hqk,khd->qhd/dot_general | solution.py:46
  125.0 21.1 %all_to_all.8 = bf16[2,512,256]{2,0,1:T(2,128)(2,1)S(1)} all-to-all(bf16[2,512,256]{2,0,1:T(2,128)(2,1)S(1)} %copy.83), channel_id=1, replica_groups=mesh['seq'=8,'res'=16] {'seq','res'}, dimensions={1} | all-to-all | bytes 1048576 | tf_op jit(solution)/shard_map/all_to_all | solution.py:103
  149.4 2.6 fusion.82
  154.9 2.6 fusion.83
  157.5 4.2 %fusion.9 = f32[4,8,32,256]{3,2,1,0:T(8,128)S(1)} fusion(bf16[256,4,8,32]{0,3,2,1:T(8,128)(2,1)S(1)} %bitcast.153, f32[4,8,256]{2,1,0:T(8,128)S(1)} %fusion.83, bf16[256,4,8,32]{0,3,2,1:T(8,128)(2,1)} %bitcast.155, bf16[256,4,8,32]{0,3,2,1:T(8,128)(2,1)S(1)} %bitcast.152), kind=kOutput, calls=%fused_computation.20 | convolution fusion | flops 274735360 | bytes 2654208 | tf_op jit(solution)/shard_map/ihst,tihd->sihd/dot_general | solution.py:62
  165.3 2.3 convert_reduce_fusion
  169.1 30.8 %all-gather.5.cloned.1.call-done = bf16[256,64,64]{0,2,1:T(8,128)(2,1)} async-done(((bf16[256,4,64]{0,2,1:T(8,128)(2,1)}), bf16[256,64,64]{0,2,1:T(8,128)(2,1)}) %all-gather.5.cloned.1.call-update) | async-done | bytes 2097168 | tf_op jit(solution)/shard_map/all_gather | solution.py:124
  199.9 2.3 slice_select_fusion
  203.3 82.5 %all-reduce.2.cloned.1.call-done = bf16[256,64,32]{0,2,1:T(8,128)(2,1)} async-done(((bf16[256,64,32]{0,2,1:T(8,128)(2,1)}), bf16[256,64,32]{0,2,1:T(8,128)(2,1)}) %all-reduce.2.cloned.1.call-update) | async-done | bytes 1048592 | tf_op jit(solution)/shard_map/psum | solution.py:14
  285.8 6.8 %fusion.8 = bf16[32,32,32,32]{2,3,0,1:T(8,128)(2,1)} fusion(bf16[256,64,64]{0,2,1:T(8,128)(2,1)} %all-gather.5.cloned.1.call-done, bf16[256,64,32]{0,2,1:T(8,128)(2,1)} %all-reduce.2.cloned.1.call-done, s32[]{:T(128)S(6)} %select_n.26), kind=kOutput, calls=%fused_computation.18 | convolution fusion | flops 538968064 | bytes 3145732 | tf_op jit(solution)/shard_map/sic,sjd->ijcd/dot_general | solution.py:137
  292.5 12.0 %copy.97 = bf16[32,32,32,32]{3,2,1,0:T(8,128)(2,1)} copy(bf16[32,32,32,32]{2,3,0,1:T(8,128)(2,1)} %fusion.8) | data formatting | bytes 4194304 | tf_op jit(solution)/shard_map/convert_element_type | solution.py:140
  304.5 11.3 %reshape.151 = bf16[32,32,1024]{2,1,0:T(8,128)(2,1)S(1)} reshape(bf16[32,32,32,32]{3,2,1,0:T(8,128)(2,1)} %copy.97) | data formatting | bytes 4194304 | tf_op jit(solution)/shard_map/reshape | solution.py:140
  315.9 6.8 %fusion.7 = bf16[32,32,32,32]{2,3,0,1:T(8,128)(2,1)} fusion(bf16[256,64,64]{0,2,1:T(8,128)(2,1)} %all-gather.5.cloned.1.call-done, bf16[256,64,32]{0,2,1:T(8,128)(2,1)} %all-reduce.2.cloned.1.call-done, s32[]{:T(128)S(6)} %select_n.26), kind=kOutput, calls=%fused_computation.17 | convolution fusion | flops 538968064 | bytes 3145732 | tf_op jit(solution)/shard_map/sic,sjd->ijcd/dot_general | solution.py:137
  322.7 12.0 %copy.96 = bf16[32,32,32,32]{3,2,1,0:T(8,128)(2,1)} copy(bf16[32,32,32,32]{2,3,0,1:T(8,128)(2,1)} %fusion.7) | data formatting | bytes 4194304 | tf_op jit(solution)/shard_map/convert_element_type | solution.py:140
  334.7 12.5 %reshape.150 = bf16[32,32,1024]{2,1,0:T(8,128)(2,1)} reshape(bf16[32,32,32,32]{3,2,1,0:T(8,128)(2,1)} %copy.96) | data formatting | bytes 4194304 | tf_op jit(solution)/shard_map/reshape | solution.py:140
  (91 shorter events, 32.9 us)
Async XLA Ops:
  7.2 63.7 %copy-start = (bf16[256,1024]{1,0:T(8,128)(2,1)S(1)}, bf16[256,1024]{1,0:T(8,128)(2,1)}, u32[]{:S(2)}) copy-start(bf16[256,1024]{1,0:T(8,128)(2,1)} %param.16) | copy-start | bytes 1572868
  7.2 86.3 %all-gather.3.cloned.1.call-start = ((), (), s32[]{:S(2)}) async-start(), calls=%async_computation.2 | async-start | bytes 4456448 | tf_op jit(solution)/shard_map/all_gather | solution.py:92
  46.7 22.9 %all-to-all-start = ((bf16[32,32,256]{2,1,0:T(8,128)(2,1)}), bf16[32,32,256]{2,1,0:T(8,128)(2,1)S(1)}, u32[]{:S(2)}, u32[]{:S(2)}) async-start(bf16[32,32,256]{2,1,0:T(8,128)(2,1)} %param.13), calls=%async_computation | async-start | bytes 1048576 | tf_op jit(solution)/shard_map/all_to_all | solution.py:82
  58.6 141.3 %all-gather.5.cloned.1.call-start = ((), (), s32[]{:S(2)}) async-start(), calls=%async_computation.3 | async-start | bytes 2228224 | tf_op jit(solution)/shard_map/all_gather | solution.py:124
  69.6 2.0 copy-start.3
  71.6 1.9 copy-start.2
  99.0 23.1 %copy-start.9 = (bf16[256,256]{1,0:T(8,128)(2,1)S(1)}, bf16[256,256]{1,0:T(8,128)(2,1)}, u32[]{:S(2)}) copy-start(bf16[256,256]{1,0:T(8,128)(2,1)} %param.17) | copy-start | bytes 393220
  146.3 3.1 copy-start.5
  154.8 2.6 copy-start.7
  154.8 2.6 copy-start.6
  157.5 5.6 %copy-start.10 = (bf16[256,256]{1,0:T(8,128)(2,1)S(1)}, bf16[256,256]{1,0:T(8,128)(2,1)}, u32[]{:S(2)}) copy-start(bf16[256,256]{1,0:T(8,128)(2,1)} %param.19) | copy-start | bytes 393220
  161.7 3.5 copy-start.8
  165.3 2.5 copy-start.11
  168.8 117.0 %all-reduce.2.cloned.1.call-start = ((), (), s32[]{:S(2)}) async-start(), calls=%async_computation.4 | async-start | bytes 2097152 | tf_op jit(solution)/shard_map/psum | solution.py:14
  334.7 12.5 %copy-start.4 = (bf16[1024,128]{1,0:T(8,128)(2,1)S(1)}, bf16[1024,128]{1,0:T(8,128)(2,1)}, u32[]{:S(2)}) copy-start(bf16[1024,128]{1,0:T(8,128)(2,1)} %param.23) | copy-start | bytes 786436
  334.7 16.3 %copy-start.1 = (bf16[256,1024]{1,0:T(8,128)(2,1)S(1)}, bf16[256,1024]{1,0:T(8,128)(2,1)}, u32[]{:S(2)}) copy-start(bf16[256,1024]{1,0:T(8,128)(2,1)} %param.16) | copy-start | bytes 1572868
Sparse Core Ops, SparseCore 0:
  46.8 46.6 all-gather.2
  168.9 30.9 all-gather.4
  202.4 83.3 all-reduce.1
where the time goes:
time: 363 us; the launch traced here: 358 us
  waiting for transfers between devices  144 us (40%)
  local copies, waits for them, and re-layouts  65.3 us (18%)
  matrix products  56.3 us (16%)
  blocking collectives  53.8 us (15%)
  between operations  14.2 us (4%)
  starting transfers between devices  12.5 us (3%)
  other arithmetic  11.7 us (3%)
    psum x1, waiting for transfers between devices, from_root(): return lax.psum(kept, axis)  82.5 us
    all_gather x1, blocking collectives, body(): column_bias = lax.all_gather(tile_bias, 'seq', axis=1, tiled=True)  32.7 us
    all_gather x1, waiting for transfers between devices, body(): row_side = lax.all_gather(factors, 'res', axis=1, tiled=True)  30.8 us
    convert_element_type x2, local copies, waits for them, and re-layouts, body(): outer_sum.astype(jnp.bfloat16)  24 us
    reshape x2, local copies, waits for them, and re-layouts, body(): outer_sum.astype(jnp.bfloat16)  23.8 us
    all_to_all x1, blocking collectives, body(): lax.all_to_all(row_alignment_state, ('seq', 'res'), split_axis=1, concat_...  21.1 us
    all_gather x1, waiting for transfers between devices, body(): full_bias = lax.all_gather(column_bias, 'res', axis=2, tiled=True)  19.7 us
    dot_general x2, matrix products, body(): jnp.einsum('sic,sjd->ijcd', left_block, right_cols, preferred_element_typ...  13.6 us
  transfers between devices with their start and end apart: 4, of which 4 were waited for; matrix products, arithmetic and copies ran while one was open for 1% of the time, Pallas kernels for 0%

commit v1 on v0

v1 whole, which is shorter than its diff:
```python
import functools

import jax
import jax.numpy as jnp
from jax import lax
from jax.experimental import pallas as pl
from jax.experimental.pallas import tpu as pltpu
from jax.sharding import PartitionSpec as P

H = 8
D = 32
C = 256
SEQ = 8
RES = 16
EPS = 1e-05
MESH = pl.DeviceIdType.MESH
F32 = jnp.float32
BF16 = jnp.bfloat16
ANY = pl.BlockSpec(memory_space=pl.ANY)
VMEM = pl.BlockSpec(memory_space=pltpu.VMEM)
NT = (((1,), (1,)), ((), ()))
TN = (((0,), (0,)), ((), ()))


def layer_norm(values):
    center = values - jnp.mean(values, axis=-1, keepdims=True)
    spread = jnp.mean(center * center, axis=-1, keepdims=True)
    return center * lax.rsqrt(spread + EPS)


def dot(a, b):
    return jnp.dot(a, b, preferred_element_type=F32)


def dot_nt(a, b):
    return lax.dot_general(a, b, NT, preferred_element_type=F32)


def dot_tn(a, b):
    return lax.dot_general(a, b, TN, preferred_element_type=F32)


def bias_kernel(pair_ref, weight_ref, out_ref):
    lane = lax.broadcasted_iota(jnp.int32, (32, 512), 1) % 64
    weight = weight_ref[...]

    def step(k, total):
        rows = pair_ref[pl.ds(k * 8, 8)].reshape(256, 128).astype(F32)
        spread = dot(layer_norm(rows).astype(BF16), weight)
        for one in range(8):
            total = jnp.where(lane == k * 8 + one, spread[one * 32 : one * 32 + 32], total)
        return total

    total = lax.fori_loop(0, 8, step, jnp.zeros((32, 512), F32)).astype(BF16)
    for t in range(4):
        out_ref[t] = total[:, t * 128 : t * 128 + 128]


def pair_bias(pair_state, bias_weight):
    weight = jnp.repeat(bias_weight, 64, axis=1)
    return pl.pallas_call(
        bias_kernel,
        out_shape=jax.ShapeDtypeStruct((4, 32, 128), BF16),
        in_specs=[VMEM, VMEM],
        out_specs=VMEM,
        compiler_params=pltpu.CompilerParams(vmem_limit_bytes=32 << 20),
        name="pair_bias",
    )(pair_state, weight)


def project(x, wt_ref, wk_ref):
    proj = dot_nt(wt_ref[...], x)
    q = (proj[:C] * D ** (-0.5)).astype(BF16)
    v = proj[C : 2 * C].astype(BF16)
    g = jax.nn.sigmoid(proj[2 * C :]).astype(BF16)
    k = dot(x, wk_ref[...]).astype(BF16)
    return q, k, v, g


def row_kernel(x_ref, bias_ref, wt_ref, wk_ref, wo_ref, out_ref, qd, kk, vt, gt, mask, mid, mix):
    row = lax.broadcasted_iota(jnp.int32, (C, 512), 0) // D
    lane = lax.broadcasted_iota(jnp.int32, (C, 512), 1) // 64
    mask[...] = jnp.where(row == lane, 1.0, 0.0).astype(BF16)
    low = lax.broadcasted_iota(jnp.int32, (C, 128), 1) < 64

    for n in range(2):
        x = x_ref[:, n].reshape(512, C).astype(F32)
        q, k, v, g = project(layer_norm(x).astype(BF16), wt_ref, wk_ref)
        kk[n] = k
        vt[n] = v
        for t in range(4):
            gt[n, t] = g[:, t * 128 : t * 128 + 128]
            tile = q[:, t * 128 : t * 128 + 128].astype(F32)
            other = pltpu.roll(tile, 64, axis=1)
            qd[n, 2 * t] = jnp.where(low, tile, other).astype(BF16)
            qd[n, 2 * t + 1] = jnp.where(low, other, tile).astype(BF16)

    low32 = lax.broadcasted_iota(jnp.int32, (D, 128), 1) < 64

    def step(index, carry):
        n = index // 4
        sp = index % 4
        halves = []
        for e in range(2):
            s = sp * 2 + e
            tile = qd[n, s]
            wide = jnp.concatenate([tile] * 4, axis=1) * mask[...]
            bias = jnp.concatenate([bias_ref[t, s] for t in range(4)], axis=1)
            score = dot(kk[n], wide) + bias.astype(F32)
            peak = jnp.max(score, axis=0, keepdims=True)
            terms = jnp.exp(score - peak)
            scale = 1.0 / jnp.sum(terms, axis=0, keepdims=True)
            terms = terms.astype(BF16)
            parts = []
            for half in range(2):
                o = dot(vt[n, half * 128 : half * 128 + 128, :], terms[:, half * 256 : half * 256 + 256])
                o = o * scale[:, half * 256 : half * 256 + 256]
                for h in range(4):
                    part = o[h * D : h * D + D, (h // 2) * 128 : (h // 2) * 128 + 128]
                    if h % 2 != e:
                        part = pltpu.roll(part, 64, axis=1)
                    parts.append(part)
            halves.append(parts)
        ot = jnp.concatenate([jnp.where(low32, a, b) for a, b in zip(*halves)], axis=0)
        gated = (gt[n, sp].astype(F32) * ot).astype(BF16)
        x = x_ref[pl.ds(sp * 4, 4), n].reshape(128, C).astype(F32)
        new = x + dot_tn(gated, wo_ref[...])
        for ch in range(2):
            mid[ch] = new[:, ch * 128 : ch * 128 + 128]
        for ch in range(2):
            for a in range(4):
                mix[pl.ds(sp * 512 + n * 8 + ch * 4 + a, 32, stride=16), :] = mid[ch, pl.ds(a, 32, stride=4), :]
        return carry

    lax.fori_loop(0, 8, step, 0)
    out_ref[...] = mix[...].astype(BF16)


def row_attention(x, bias, wt, wk, wo):
    return pl.pallas_call(
        row_kernel,
        out_shape=jax.ShapeDtypeStruct((2048, 128), BF16),
        in_specs=[VMEM] * 5,
        out_specs=VMEM,
        scratch_shapes=[
            pltpu.VMEM((2, 8, C, 128), BF16),
            pltpu.VMEM((2, 512, C), BF16),
            pltpu.VMEM((2, C, 512), BF16),
            pltpu.VMEM((2, 4, C, 128), BF16),
            pltpu.VMEM((C, 512), BF16),
            pltpu.VMEM((2, 128, 128), F32),
            pltpu.VMEM((2048, 128), F32),
        ],
        compiler_params=pltpu.CompilerParams(vmem_limit_bytes=48 << 20),
        name="row_attention",
    )(x, bias, wt, wk, wo)


def column_kernel(
    x_ref, wt_ref, wk_ref, wo_ref, win_ref, wout_ref, wl_ref, wr_ref,
    out_ref, left_ref, right_ref, mix, ot, right,
):
    mix[...] = x_ref[...].astype(F32)
    head = lax.broadcasted_iota(jnp.int32, (C, C), 0) // D
    right[...] = jnp.zeros_like(right)

    def step(a, carry):
        cells = jnp.concatenate(
            [
                jnp.concatenate([mix[pl.ds(n * 8 + ch * 4 + a, 128, stride=16), :] for ch in range(2)], axis=1)
                for n in range(2)
            ],
            axis=0,
        )
        q, k, v, g = project(layer_norm(cells).astype(BF16), wt_ref, wk_ref)
        for h in range(H):
            one = jnp.where(head == h, q, jnp.zeros_like(q))
            score = dot(k, one)
            peak = jnp.max(score, axis=0, keepdims=True)
            terms = jnp.exp(score - peak)
            scale = 1.0 / jnp.sum(terms, axis=0, keepdims=True)
            ot[h * D : h * D + D, :] = dot(v[h * D : h * D + D], terms.astype(BF16)) * scale
        gated = (g.astype(F32) * ot[...]).astype(BF16)
        stream = cells + dot_tn(gated, wo_ref[...])
        normed = layer_norm(stream).astype(BF16)
        hidden = jnp.maximum(dot(normed, win_ref[...]), 0.0).astype(BF16)
        new = (stream + dot(hidden, wout_ref[...])).astype(BF16).astype(F32)
        for n in range(2):
            for ch in range(2):
                mix[pl.ds(n * 8 + ch * 4 + a, 128, stride=16), :] = new[
                    n * 128 : n * 128 + 128, ch * 128 : ch * 128 + 128
                ]
        factor = layer_norm(new).astype(BF16)
        left_ref[pl.ds(pl.multiple_of(a * D, D), D), :] = dot_nt(wl_ref[...], factor).astype(BF16)
        right[...] += dot(factor, wr_ref[a])
        return carry

    lax.fori_loop(0, 4, step, 0)
    out_ref[...] = mix[...].astype(BF16)
    right_ref[...] = right[...].astype(BF16)


def column_part(x, wt, wk, wo, win, wout, wl, wr):
    return pl.pallas_call(
        column_kernel,
        out_shape=(
            jax.ShapeDtypeStruct((2048, 128), BF16),
            jax.ShapeDtypeStruct((128, 256), BF16),
            jax.ShapeDtypeStruct((256, 128), BF16),
        ),
        in_specs=[VMEM] * 8,
        out_specs=(VMEM, VMEM, VMEM),
        scratch_shapes=[
            pltpu.VMEM((2048, 128), F32),
            pltpu.VMEM((C, 256), F32),
            pltpu.VMEM((256, 128), F32),
        ],
        compiler_params=pltpu.CompilerParams(vmem_limit_bytes=48 << 20),
        name="column_part",
    )(x, wt, wk, wo, win, wout, wl, wr)


def outer_kernel(left_ref, right_ref, w_ref, out_ref, left, wide, block, pairs):
    for n in range(2):
        left[n] = left_ref[:, :, n * 128 : n * 128 + 128].reshape(2048, 128).astype(F32)
    block[...] = jnp.zeros_like(block)
    for c in range(32):
        one = w_ref[c * 32 : c * 32 + 32, :]
        for j in range(4):
            block[c * 128 + j * 32 : c * 128 + j * 32 + 32, j * 128 : j * 128 + 128] = one
    right = jnp.concatenate([right_ref[o] for o in range(8)], axis=1)
    for c in range(0, 32, 2):
        rows = jnp.concatenate(
            [
                jnp.concatenate([left[n, pl.ds(c + k, 64, stride=32), :] for n in range(2)], axis=1)
                for k in range(2)
            ],
            axis=0,
        )
        product = (dot(rows.astype(BF16), right) * (1.0 / 256)).astype(BF16)
        for k in range(2):
            for g in range(8):
                wide[g * 64 : g * 64 + 64, (c + k) * 128 : (c + k) * 128 + 128] = product[
                    k * 64 : k * 64 + 64, g * 128 : g * 128 + 128
                ]
    update = dot(wide[...], block[...])
    for g in range(8):
        for j in range(4):
            pairs[pl.ds(g * 4 + j, 64, stride=32), :] = update[g * 64 : g * 64 + 64, j * 128 : j * 128 + 128]
    out_ref[...] = pairs[...].astype(BF16)


def outer_part(left, right, w):
    return pl.pallas_call(
        outer_kernel,
        out_shape=jax.ShapeDtypeStruct((2048, 128), BF16),
        in_specs=[VMEM] * 3,
        out_specs=VMEM,
        scratch_shapes=[
            pltpu.VMEM((2, 2048, 128), F32),
            pltpu.VMEM((512, 4096), BF16),
            pltpu.VMEM((4096, 512), BF16),
            pltpu.VMEM((2048, 128), F32),
        ],
        compiler_params=pltpu.CompilerParams(vmem_limit_bytes=48 << 20),
        name="outer_part",
    )(left, right, w)


def split_weight(weight):
    q, k, v, g = (weight[:, i * C : i * C + C] for i in range(4))
    return jnp.concatenate([q, v, g], axis=1).T, k


def split_outer(weight):
    left, right = weight[:, :D].T, weight[:, D:]
    return left, jnp.stack([jnp.pad(right, ((0, 0), (a * D, 96 - a * D))) for a in range(4)])


def me():
    return lax.axis_index("seq"), lax.axis_index("res")


def device(x, y, z, core):
    return (x * 2 + y // 2, (y % 2) * 8 + z * 2 + core)


def remote(src, dst, send, recv, target):
    return pltpu.make_async_remote_copy(
        src_ref=src, dst_ref=dst, send_sem=send, recv_sem=recv, device_id=target, device_id_type=MESH
    )


ORDERS = ("zyx", "xzy", "yxz", "zyx")


def gather_kernel(x_ref, own_ref, xo_ref, bo_ref, send, recv, ssend, srecv, xsend, xrecv, lsem):
    s, r = me()
    pos = {"x": s // 2, "y": (s % 2) * 2 + r // 8, "z": (r % 8) // 2}
    core = r % 2

    def near(dim, by):
        at = dict(pos)
        at[dim] = (pos[dim] + by) % 4
        return device(at["x"], at["y"], at["z"], core)

    sibling = (s, r + 1 - 2 * core)
    barrier = pltpu.get_barrier_semaphore()

    def greet(k, carry):
        pl.semaphore_signal(barrier, inc=1, device_id=(s, (r + k) % 16), device_id_type=MESH)
        return carry

    lax.fori_loop(1, 16, greet, 0)
    for dim in "xy":
        for by in (1, 3):
            pl.semaphore_signal(barrier, inc=1, device_id=near(dim, by), device_id_type=MESH)
    pl.semaphore_wait(barrier, 19)

    def box(t, known, dim, at, rows):
        index = [t]
        for d in "xyz":
            index.append(pl.ds(0, 4) if d in known else (at if d == dim else pos[d]))
        return bo_ref.at[(*index, core, rows)]

    everything = pl.ds(0, 32)
    started = []

    def ring(t, phase, k, src, dst, target):
        copy = remote(src, dst, send.at[t, phase, k], recv.at[t, phase, k], target)
        copy.start()
        started.append(copy)
        return copy

    def share(t, k, src, dst):
        copy = remote(src, dst, ssend.at[t, k], srecv, sibling)
        copy.start()
        started.append(copy)

    local = pltpu.make_async_copy(own_ref, bo_ref.at[:, pos["x"], pos["y"], pos["z"], core], lsem.at[0])
    local.start()
    keep = pltpu.make_async_copy(x_ref.at[r], xo_ref.at[r], lsem.at[1])
    keep.start()

    for phase in range(3):
        first = {}
        for t in range(4):
            dim, known = ORDERS[t][phase], ORDERS[t][:phase]
            mine = box(t, known, dim, pos[dim], everything)
            src = own_ref.at[t] if phase == 0 else mine
            for k, by in enumerate((1, 3)):
                first[t, k] = ring(t, phase, k, src, mine, near(dim, by))
            if phase == 0:
                share(t, 0, src, mine)
        if phase == 0:

            def scatter(k, carry):
                to = (r + k) % 16
                remote(x_ref.at[to], xo_ref.at[r], xsend, xrecv, (s, to)).start()
                return carry

            lax.fori_loop(1, 16, scatter, 0)
        second = {}
        for t in range(4):
            dim, known = ORDERS[t][phase], ORDERS[t][:phase]
            for k, by in enumerate((1, 3)):
                first[t, k].wait_recv()
                at = (pos[dim] + (3, 1)[k]) % 4
                rows = pl.ds(16 * k, 16)
                part = box(t, known, dim, at, rows)
                second[t, k] = ring(t, phase, 2 + k, part, part, near(dim, by))
                whole = box(t, known, dim, at, everything)
                share(t, 1 + phase * 4 + k, whole, whole)
        for t in range(4):
            dim, known = ORDERS[t][phase], ORDERS[t][:phase]
            for k in range(2):
                second[t, k].wait_recv()
                part = box(t, known, dim, (pos[dim] + 2) % 4, pl.ds(16 * k, 16))
                share(t, 3 + phase * 4 + k, part, part)
        if phase == 0:
            local.wait()
    keep.wait()
    for copy in started:
        copy.wait_send()
    half = bo_ref.at[:, :, :, :, 0]
    remote(half, half, lsem.at[0], srecv, sibling).wait_recv()
    most = xo_ref.at[pl.ds(0, 15)]
    remote(most, most, xsend, xrecv, sibling).wait()


def gather(x, own):
    return pl.pallas_call(
        gather_kernel,
        out_shape=(
            jax.ShapeDtypeStruct((16, 2, 32, C), BF16),
            jax.ShapeDtypeStruct((4, 4, 4, 4, 2, 32, 128), BF16),
        ),
        in_specs=[ANY, ANY],
        out_specs=(ANY, ANY),
        scratch_shapes=[
            pltpu.SemaphoreType.DMA((4, 3, 4)),
            pltpu.SemaphoreType.DMA((4, 3, 4)),
            pltpu.SemaphoreType.DMA((4, 13)),
            pltpu.SemaphoreType.DMA,
            pltpu.SemaphoreType.DMA,
            pltpu.SemaphoreType.DMA,
            pltpu.SemaphoreType.DMA((2,)),
        ],
        compiler_params=pltpu.CompilerParams(collective_id=0, has_side_effects=True),
        name="gather",
    )(x, own)


def exchange_kernel(x_ref, out_ref, send, recv, lsem):
    s, r = me()
    here = s * RES + r
    barrier = pltpu.get_barrier_semaphore()

    def greet(k, carry):
        to = (here + k) % 128
        pl.semaphore_signal(barrier, inc=1, device_id=(to // RES, to % RES), device_id_type=MESH)
        return carry

    lax.fori_loop(1, 128, greet, 0)
    keep = pltpu.make_async_copy(x_ref.at[here], out_ref.at[here], lsem)
    keep.start()
    pl.semaphore_wait(barrier, 127)

    def scatter(k, carry):
        to = (here + k) % 128
        remote(x_ref.at[to], out_ref.at[here], send, recv, (to // RES, to % RES)).start()
        return carry

    lax.fori_loop(1, 128, scatter, 0)
    keep.wait()
    most = out_ref.at[pl.ds(0, 127)]
    remote(most, most, send, recv, (s, (r + 1) % RES)).wait()


def exchange(x):
    return pl.pallas_call(
        exchange_kernel,
        out_shape=jax.ShapeDtypeStruct((128, 16, 128), BF16),
        in_specs=[ANY],
        out_specs=ANY,
        scratch_shapes=[pltpu.SemaphoreType.DMA] * 3,
        compiler_params=pltpu.CompilerParams(collective_id=1, has_side_effects=True),
        name="exchange",
    )(x.reshape(128, 16, 128)).reshape(2048, 128)


def factors_kernel(left_ref, right_ref, lo_ref, ro_ref, lsend, lrecv, fsend, frecv, rsend, rrecv, own):
    s, r = me()
    core = r % 2
    chip = r // 2
    sibling = (s, r + 1 - 2 * core)
    column = 2 * s + r // 8
    source = r // 2
    barrier = pltpu.get_barrier_semaphore()

    def greet(k, carry):
        pl.semaphore_signal(barrier, inc=1, device_id=(s, (r + k) % 16), device_id_type=MESH)
        return carry

    lax.fori_loop(1, 16, greet, 0)
    is_own = column == r

    def greet_right(o, carry):
        owner = (r % 2) * 8 + o

        @pl.when(jnp.logical_or(source != s, owner != r))
        def _():
            pl.semaphore_signal(barrier, inc=1, device_id=(source, owner), device_id_type=MESH)

        return carry

    lax.fori_loop(0, 8, greet_right, 0)
    pl.semaphore_wait(barrier, 15 + 8 - jnp.where(is_own, 1, 0))

    keep = pltpu.make_async_copy(left_ref, lo_ref.at[r], own)
    keep.start()
    to_sibling = remote(left_ref, lo_ref.at[r], fsend, frecv, sibling)
    to_sibling.start()
    copies = []
    for k in range(1, 8):
        copy = remote(left_ref, lo_ref.at[r], lsend.at[k], lrecv.at[k], (s, ((chip + k) % 8) * 2 + core))
        copy.start()
        copies.append(copy)

    def send_right(k, carry):
        to = (s + k) % 8

        @pl.when(jnp.logical_not(jnp.logical_and(is_own, k == 0)))
        def _():
            remote(right_ref, ro_ref.at[r % 8], rsend, rrecv, (to, column)).start()

        return carry

    lax.fori_loop(0, 8, send_right, 0)
    keep.wait()

    @pl.when(is_own)
    def _():
        mine = pltpu.make_async_copy(right_ref, ro_ref.at[r % 8], own)
        mine.start()
        mine.wait()

    for k in range(1, 8):
        copies[k - 1].wait_recv()
        got = lo_ref.at[((chip + 8 - k) % 8) * 2 + core]
        remote(got, got, fsend, frecv, sibling).start()
    for copy in copies:
        copy.wait_send()
    half = lo_ref.at[pl.ds(0, 8)]
    remote(half, half, fsend, frecv, sibling).wait()

    @pl.when(is_own)
    def _():
        most = ro_ref.at[pl.ds(0, 7)]
        remote(most, most, rsend, rrecv, sibling).wait()

    @pl.when(jnp.logical_not(is_own))
    def _():
        remote(ro_ref, ro_ref, rsend, rrecv, sibling).wait()


def share_factors(left, right):
    return pl.pallas_call(
        factors_kernel,
        out_shape=(
            jax.ShapeDtypeStruct((16, 128, 256), BF16),
            jax.ShapeDtypeStruct((8, 256, 128), BF16),
        ),
        in_specs=[ANY, ANY],
        out_specs=(ANY, ANY),
        scratch_shapes=[
            pltpu.SemaphoreType.DMA((8,)),
            pltpu.SemaphoreType.DMA((8,)),
        ]
        + [pltpu.SemaphoreType.DMA] * 5,
        compiler_params=pltpu.CompilerParams(collective_id=2, has_side_effects=True),
        name="share_factors",
    )(left, right)


def body(
    alignment,
    pair_state,
    bias_weight,
    row_weight,
    row_output_weight,
    column_weight,
    column_output_weight,
    transition_in,
    transition_out,
    outer_in,
    outer_out,
):
    own = pair_bias(pair_state, bias_weight)
    x, bias = gather(alignment.reshape(16, 2, 32, C), own)
    wt, wk = split_weight(row_weight)
    mid = row_attention(x, bias.reshape(4, 8, 512, 128), wt, wk, row_output_weight)
    cells = exchange(mid)
    wt, wk = split_weight(column_weight)
    wl, wr = split_outer(outer_in)
    new, left, right = column_part(
        cells, wt, wk, column_output_weight, transition_in, transition_out, wl, wr
    )
    left, right = share_factors(left, right)
    pair_update = outer_part(left, right, outer_out).reshape(64, 32, 128)
    alignment_out = new.reshape(128, 2, 2, 4, 128).transpose(0, 1, 3, 2, 4).reshape(256, 4, C)
    return (alignment_out, pair_update)


def solution(mesh):
    in_specs = (P("seq", "res", None), P("seq", "res", None)) + (P(),) * 9
    out_specs = (P(None, ("seq", "res"), None), P("seq", "res", None))
    return jax.shard_map(body, mesh=mesh, in_specs=in_specs, out_specs=out_specs, check_vma=False)
```

time: 363 us -> 132 us (0.36)
  waiting for transfers between devices: 144 us -> 0 us
  Pallas kernels: 0 us -> 115 us
  matrix products: 56.3 us -> 0 us
  blocking collectives: 53.8 us -> 0 us
  local copies, waits for them, and re-layouts: 65.3 us -> 13.8 us
  between operations: 14.2 us -> 0.9 us
  starting transfers between devices: 12.5 us -> 0 us
  other arithmetic: 11.7 us -> 0.09 us
    pallas_call x0 -> x7, Pallas kernels: none -> 115 us  [the longest x1 39.5 us: gather(): pl.pallas_call(gather_kernel, out_shape=(jax.ShapeDtypeStruct((16, 2, 32,...]
    psum x1 -> x0, waiting for transfers between devices: 82.5 us -> none  [from_root(): return lax.psum(kept, axis)]
    all_gather x2 -> x0, waiting for transfers between devices: 50.5 us -> none  [the longest x1 30.8 us: body(): row_side = lax.all_gather(factors, 'res', axis=1, tiled=True)]
    dot_general x14 -> x0, matrix products: 44.9 us -> none  [the longest x2 13.6 us: body(): jnp.einsum('sic,sjd->ijcd', left_block, right_cols, preferred_element_typ...]
    all_gather x1 -> x0, blocking collectives: 32.7 us -> none  [body(): column_bias = lax.all_gather(tile_bias, 'seq', axis=1, tiled=True)]
    convert_element_type x7 -> x0, local copies, waits for them, and re-layouts: 25.4 us -> none  [the longest x2 24 us: body(): outer_sum.astype(jnp.bfloat16)]
    reshape x3 -> x1, local copies, waits for them, and re-layouts: 25.1 us -> 0.11 us  [pair_bias(): weight = jnp.repeat(bias_weight, 64, axis=1)]
    all_to_all x1 -> x0, blocking collectives: 21.1 us -> none  [body(): lax.all_to_all(row_alignment_state, ('seq', 'res'), split_axis=1, concat_...]
  transfers between devices with their start and end apart: 4 -> 0, of which waited for: 4 -> 0; matrix products, arithmetic and copies ran while one was open for 1% -> 0% of each run, Pallas kernels for 0% -> 0%
where the time goes in v1:
time: 132 us; the launch traced here: 130 us
  Pallas kernels  115 us (87%)
  local copies, waits for them, and re-layouts  13.8 us (10%)
    pallas_call x1, Pallas kernels, gather(): pl.pallas_call(gather_kernel, out_shape=(jax.ShapeDtypeStruct((16, 2, 32,...  39.5 us
    pallas_call x1, Pallas kernels, share_factors(): pl.pallas_call(factors_kernel, out_shape=(jax.ShapeDtypeStruct((16, 128,...  19.4 us
    pallas_call x1, Pallas kernels, exchange(): pl.pallas_call(exchange_kernel, out_shape=jax.ShapeDtypeStruct((128, 16,...  16.6 us
    pallas_call x1, Pallas kernels, column_part(): pl.pallas_call(column_kernel, out_shape=(jax.ShapeDtypeStruct((2048, 128)...  16 us
    pallas_call x1, Pallas kernels, row_attention(): pl.pallas_call(row_kernel, out_shape=jax.ShapeDtypeStruct((2048, 128), BF...  12.8 us
    unnamed x39, local copies, waits for them, and re-layouts  10.8 us
    pallas_call x1, Pallas kernels, outer_part(): pl.pallas_call(outer_kernel, out_shape=jax.ShapeDtypeStruct((2048, 128),...  7.04 us
    pallas_call x1, Pallas kernels, pair_bias(): pl.pallas_call(bias_kernel, out_shape=jax.ShapeDtypeStruct((4, 32, 128),...  3.25 us

profile of v1, /device:TPU:1, one launch (start us, length us, event | category | flops | bytes accessed | tf_op | source)
XLA Modules:
  0.0 129.6 jit_solution(2251164519046445043)
XLA Ops:
  0.6 0.7 broadcast_in_dim.3
  1.5 1.0 copy-done.7
  2.5 3.2 %pair_bias.1.own_ref = bf16[4,32,128]{2,1,0:T(8,128)(2,1)S(1)} custom-call(bf16[64,32,128]{2,1,0:T(8,128)(2,1)S(1)} %copy-done.7, bf16[128,512]{1,0:T(8,128)(2,1)S(1)} %copy.20.weight_ref), custom_call_target="tpu_custom_call" | custom-call | tf_op jit(solution)/shard_map/pair_bias/pallas_call | solution.py:61
  5.8 0.6 copy-done.12
  6.4 39.5 %gather.1 = (bf16[16,2,32,256]{3,2,1,0:T(8,128)(2,1)}, bf16[4,4,4,4,2,32,128]{6,5,4,3,2,1,0:T(8,128)(2,1)}) custom-call(bf16[16,2,32,256]{3,2,1,0:T(8,128)(2,1)} %bitcast.28, bf16[4,32,128]{2,1,0:T(8,128)(2,1)} %copy-done.12), custom_call_target="tpu_custom_call" | custom-call | tf_op jit(solution)/shard_map/gather/pallas_call | solution.py:392
  46.0 1.0 slice.29
  46.9 0.1 copy.28
  47.1 1.0 fusion.1
  48.2 2.2 %copy-done = bf16[4,4,4,4,2,32,128]{6,5,4,3,2,1,0:T(8,128)(2,1)S(1)} copy-done((bf16[4,4,4,4,2,32,128]{6,5,4,3,2,1,0:T(8,128)(2,1)S(1)}, bf16[4,4,4,4,2,32,128]{6,5,4,3,2,1,0:T(8,128)(2,1)}, u32[]{:S(2)}) %copy-start) | copy-done | bytes 4194328
  50.5 1.0 copy-done.6
  51.5 12.8 %row_attention.1 = bf16[2048,128]{1,0:T(8,128)(2,1)S(1)} custom-call(bf16[16,2,32,256]{3,2,1,0:T(8,128)(2,1)S(1)} %copy-done.6, bf16[4,8,512,128]{3,2,1,0:T(8,128)(2,1)S(1)} %bitcast.25, bf16[768,256]{1,0:T(8,128)(2,1)S(1)} %maximum_bitcast_fusion.wt_ref, bf16[256,256]{1,0:T(8,128)(2,1)S(1)} %get-tuple-element.18.wk_ref, bf16[256,256]{1,0:T(8,128)(2,1)S(1)} %copy-done.10), custom_call_target="tpu_custom_call" | custom-call | tf_op jit(solution)/shard_map/row_attention/pallas_call | solution.py:140
  64.4 0.8 copy-done.2
  65.2 16.6 %exchange.1 = bf16[128,16,128]{2,1,0:T(8,128)(2,1)} custom-call(bf16[128,16,128]{2,1,0:T(8,128)(2,1)} %bitcast.27), custom_call_target="tpu_custom_call" | custom-call | tf_op jit(solution)/shard_map/exchange/pallas_call | solution.py:441
  81.8 0.1 copy.30
  82.2 0.1 copy.31
  82.3 0.1 pad_bitcast_fusion.3
  82.5 1.0 copy-done.1
  83.5 16.0 %column_part.1 = (bf16[2048,128]{1,0:T(8,128)(2,1)}, bf16[128,256]{1,0:T(8,128)(2,1)S(1)}, bf16[256,128]{1,0:T(8,128)(2,1)S(1)}) custom-call(bf16[2048,128]{1,0:T(8,128)(2,1)S(1)} %bitcast.26, bf16[768,256]{1,0:T(8,128)(2,1)S(1)} %maximum_bitcast_fusion.1.wt_ref, bf16[256,256]{1,0:T(8,128)(2,1)S(1)} %get-tuple-element.16.wk_ref, ...), custom_call_target="tpu_custom_call" | custom-call | tf_op jit(solution)/shard_map/column_part/pallas_call | solution.py:204
  99.6 0.6 copy-done.13
  100.2 0.6 copy-done.14
  100.8 19.4 %share_factors.1 = (bf16[16,128,256]{2,1,0:T(8,128)(2,1)}, bf16[8,256,128]{2,1,0:T(8,128)(2,1)}) custom-call(bf16[128,256]{1,0:T(8,128)(2,1)} %copy-done.13, bf16[256,128]{1,0:T(8,128)(2,1)} %copy-done.14), custom_call_target="tpu_custom_call" | custom-call | tf_op jit(solution)/shard_map/share_factors/pallas_call | solution.py:528
  120.3 1.2 copy-done.3
  121.5 1.0 copy-done.8
  122.5 7.0 %outer_part.1 = bf16[2048,128]{1,0:T(8,128)(2,1)} custom-call(bf16[16,128,256]{2,1,0:T(8,128)(2,1)S(1)} %copy-done.3, bf16[8,256,128]{2,1,0:T(8,128)(2,1)S(1)} %copy-done.8, bf16[1024,128]{1,0:T(8,128)(2,1)S(1)} %copy-done.9), custom_call_target="tpu_custom_call" | custom-call | tf_op jit(solution)/shard_map/outer_part/pallas_call | solution.py:254
  (34 shorter events, 0.5 us)
Async XLA Ops:
  0.6 47.6 %copy-start.10 = (bf16[256,256]{1,0:T(8,128)(2,1)S(1)}, bf16[256,256]{1,0:T(8,128)(2,1)}, u32[]{:S(2)}) copy-start(bf16[256,256]{1,0:T(8,128)(2,1)} %wo_ref.2) | copy-start | bytes 393220
  1.5 1.0 copy-start.7
  5.8 0.6 copy-start.12
  48.2 33.6 %slice-start = ((bf16[256,1024]{1,0:T(8,128)(2,1)}), bf16[256,512]{1,0:T(8,128)(2,1)S(1)}, s32[]{:S(2)}) async-start(bf16[256,1024]{1,0:T(8,128)(2,1)} %param.16), calls=%async_computation | async-start | bytes 524288 | tf_op jit(solution)/shard_map/slice | solution.py:271
  48.2 2.2 %copy-start = (bf16[4,4,4,4,2,32,128]{6,5,4,3,2,1,0:T(8,128)(2,1)S(1)}, bf16[4,4,4,4,2,32,128]{6,5,4,3,2,1,0:T(8,128)(2,1)}, u32[]{:S(2)}) copy-start(bf16[4,4,4,4,2,32,128]{6,5,4,3,2,1,0:T(8,128)(2,1)} %get-tuple-element.10) | copy-start | bytes 12582916
  50.4 1.0 copy-start.6
  51.5 30.5 %copy-start.15 = (bf16[256,1024]{1,0:T(8,128)(2,1)S(1)}, bf16[256,1024]{1,0:T(8,128)(2,1)}, u32[]{:S(2)}) copy-start(bf16[256,1024]{1,0:T(8,128)(2,1)} %param.16) | copy-start | bytes 1572868
  51.5 30.6 %copy-start.16 = (bf16[256,64]{0,1:T(8,128)(2,1)S(1)}, bf16[256,64]{0,1:T(8,128)(2,1)}, u32[]{:S(2)}) copy-start(bf16[256,64]{0,1:T(8,128)(2,1)} %param.20) | copy-start | bytes 98308
  51.5 31.0 %copy-start.4 = (bf16[256,1024]{1,0:T(8,128)(2,1)S(1)}, bf16[256,1024]{1,0:T(8,128)(2,1)}, u32[]{:S(2)}) copy-start(bf16[256,1024]{1,0:T(8,128)(2,1)} %win_ref.1) | copy-start | bytes 1572868
  51.5 31.0 %copy-start.5 = (bf16[1024,256]{1,0:T(8,128)(2,1)S(1)}, bf16[1024,256]{1,0:T(8,128)(2,1)}, u32[]{:S(2)}) copy-start(bf16[1024,256]{1,0:T(8,128)(2,1)} %wout_ref.1) | copy-start | bytes 1572868
  51.5 31.0 %copy-start.11 = (bf16[256,256]{1,0:T(8,128)(2,1)S(1)}, bf16[256,256]{1,0:T(8,128)(2,1)}, u32[]{:S(2)}) copy-start(bf16[256,256]{1,0:T(8,128)(2,1)} %wo_ref.3) | copy-start | bytes 393220
  64.4 0.8 copy-start.2
  65.2 55.1 %copy-start.9 = (bf16[1024,128]{1,0:T(8,128)(2,1)S(1)}, bf16[1024,128]{1,0:T(8,128)(2,1)}, u32[]{:S(2)}) copy-start(bf16[1024,128]{1,0:T(8,128)(2,1)} %w_ref.1) | copy-start | bytes 786436
  82.5 1.0 copy-start.1
  99.6 0.6 copy-start.13
  100.2 0.6 copy-start.14
  120.3 1.2 copy-start.3
  121.5 1.0 copy-start.8

commit v2 on v0

v2 whole, which is shorter than its diff:
```python
import functools

import jax
import jax.numpy as jnp
from jax import lax
from jax.experimental import pallas as pl
from jax.experimental.pallas import tpu as pltpu
from jax.sharding import PartitionSpec as P

H = 8
D = 32
C = 256
SEQ = 8
RES = 16
EPS = 1e-05
MESH = pl.DeviceIdType.MESH
F32 = jnp.float32
BF16 = jnp.bfloat16
ANY = pl.BlockSpec(memory_space=pl.ANY)
VMEM = pl.BlockSpec(memory_space=pltpu.VMEM)
NT = (((1,), (1,)), ((), ()))
TN = (((0,), (0,)), ((), ()))


def layer_norm(values):
    center = values - jnp.mean(values, axis=-1, keepdims=True)
    spread = jnp.mean(center * center, axis=-1, keepdims=True)
    return center * lax.rsqrt(spread + EPS)


def dot(a, b):
    return jnp.dot(a, b, preferred_element_type=F32)


def dot_nt(a, b):
    return lax.dot_general(a, b, NT, preferred_element_type=F32)


def dot_tn(a, b):
    return lax.dot_general(a, b, TN, preferred_element_type=F32)


def project(x, wt, wk):
    proj = dot_nt(wt, x)
    q = (proj[:C] * D ** (-0.5)).astype(BF16)
    v = proj[C : 2 * C].astype(BF16)
    g = jax.nn.sigmoid(proj[2 * C :]).astype(BF16)
    k = dot(x, wk).astype(BF16)
    return q, k, v, g


def device(x, y, z, core):
    return (x * 2 + y // 2, (y % 2) * 8 + z * 2 + core)


def remote(src, dst, send, recv, target):
    return pltpu.make_async_remote_copy(
        src_ref=src, dst_ref=dst, send_sem=send, recv_sem=recv, device_id=target, device_id_type=MESH
    )


ORDERS = ("zyx", "xzy", "yxz", "zyx")


def pair_bias(pair_ref, weight_ref, out_ref):
    lane = lax.broadcasted_iota(jnp.int32, (32, 512), 1) % 64
    low = lax.broadcasted_iota(jnp.int32, (128, 128), 1) < 64
    narrow = weight_ref[...].astype(F32)
    weight = jnp.concatenate(
        [jnp.where(low, narrow[:, 2 * t : 2 * t + 1], narrow[:, 2 * t + 1 : 2 * t + 2]) for t in range(4)], axis=1
    ).astype(BF16)

    def step(k, total):
        rows = pair_ref[pl.ds(k * 8, 8)].reshape(256, 128).astype(F32)
        spread = dot(layer_norm(rows).astype(BF16), weight)
        for one in range(8):
            total = jnp.where(lane == k * 8 + one, spread[one * 32 : one * 32 + 32], total)
        return total

    total = lax.fori_loop(0, 8, step, jnp.zeros((32, 512), F32)).astype(BF16)
    for t in range(4):
        out_ref[t] = total[:, t * 128 : t * 128 + 128]


def row_project(n, x_ref, wt, wk, qd, kk, vt, gt):
    low = lax.broadcasted_iota(jnp.int32, (C, 128), 1) < 64
    x = x_ref[:, n].reshape(512, C).astype(F32)
    q, k, v, g = project(layer_norm(x).astype(BF16), wt[...], wk)
    kk[n] = k
    vt[n] = v
    for t in range(4):
        gt[n, t] = g[:, t * 128 : t * 128 + 128]
        tile = q[:, t * 128 : t * 128 + 128].astype(F32)
        other = pltpu.roll(tile, 64, axis=1)
        qd[n, 2 * t] = jnp.where(low, tile, other).astype(BF16)
        qd[n, 2 * t + 1] = jnp.where(low, other, tile).astype(BF16)


def row_attend(n, sp, x_ref, bias_ref, wo, qd, kk, vt, gt, mask, mid, mix):
    low = lax.broadcasted_iota(jnp.int32, (D, 128), 1) < 64
    halves = []
    for e in range(2):
        tile = qd[n, sp * 2 + e]
        wide = jnp.concatenate([tile] * 4, axis=1) * mask[...]
        bias = jnp.concatenate([bias_ref[t, sp, 2 * e : 2 * e + 2].reshape(512, 128) for t in range(4)], axis=1)
        score = dot(kk[n], wide) + bias.astype(F32)
        peak = jnp.max(score, axis=0, keepdims=True)
        terms = jnp.exp(score - peak)
        scale = 1.0 / jnp.sum(terms, axis=0, keepdims=True)
        terms = terms.astype(BF16)
        parts = []
        for half in range(2):
            o = dot(vt[n, half * 128 : half * 128 + 128, :], terms[:, half * 256 : half * 256 + 256])
            o = o * scale[:, half * 256 : half * 256 + 256]
            for h in range(4):
                part = o[h * D : h * D + D, (h // 2) * 128 : (h // 2) * 128 + 128]
                if h % 2 != e:
                    part = pltpu.roll(part, 64, axis=1)
                parts.append(part)
        halves.append(parts)
    ot = jnp.concatenate([jnp.where(low, a, b) for a, b in zip(*halves)], axis=0)
    gated = (gt[n, sp].astype(F32) * ot).astype(BF16)
    x = x_ref[pl.ds(sp * 4, 4), n].reshape(128, C).astype(F32)
    new = x + dot_tn(gated, wo[...])
    for ch in range(2):
        mid[ch] = new[:, ch * 128 : ch * 128 + 128]
    for ch in range(2):
        for a in range(4):
            mix[pl.ds(sp * 512 + n * 8 + ch * 4 + a, 32, stride=16), :] = mid[ch, pl.ds(a, 32, stride=4), :]


def column_step(a, mix, wt, wk, wo, win, wout, wf, ot):
    head = lax.broadcasted_iota(jnp.int32, (C, C), 0) // D
    cells = jnp.concatenate(
        [
            jnp.concatenate([mix[pl.ds(n * 8 + ch * 4 + a, 128, stride=16), :] for ch in range(2)], axis=1)
            for n in range(2)
        ],
        axis=0,
    )
    q, k, v, g = project(layer_norm(cells).astype(BF16), wt[...], wk)
    for h in range(H):
        one = jnp.where(head == h, q, jnp.zeros_like(q))
        score = dot(k, one)
        peak = jnp.max(score, axis=0, keepdims=True)
        terms = jnp.exp(score - peak)
        scale = 1.0 / jnp.sum(terms, axis=0, keepdims=True)
        ot[h * D : h * D + D, :] = dot(v[h * D : h * D + D], terms.astype(BF16)) * scale
    gated = (g.astype(F32) * ot[...]).astype(BF16)
    stream = cells + dot_tn(gated, wo[...])
    normed = layer_norm(stream).astype(BF16)
    hidden = jnp.maximum(dot(normed, win[...]), 0.0).astype(BF16)
    new = (stream + dot(hidden, wout[...])).astype(BF16).astype(F32)
    for n in range(2):
        for ch in range(2):
            mix[pl.ds(n * 8 + ch * 4 + a, 128, stride=16), :] = new[
                n * 128 : n * 128 + 128, ch * 128 : ch * 128 + 128
            ]
    return dot_nt(wf[...], layer_norm(new).astype(BF16)).astype(BF16)


def outer_weight(w_ref, block):
    block[...] = jnp.zeros_like(block)
    for c in range(32):
        one = w_ref[c * 32 : c * 32 + 32, :]
        for j in range(4):
            block[c * 128 + j * 32 : c * 128 + j * 32 + 32, j * 128 : j * 128 + 128] = one


def outer_part(left_ref, right_ref, out_ref, left, wide, block, pairs):
    for n in range(2):
        left[n] = left_ref[:, :, :, n * 128 : n * 128 + 128].reshape(2048, 128).astype(F32)
    right = right_ref[...].reshape(1024, 256)
    for c in range(0, 32, 2):
        rows = jnp.concatenate(
            [
                jnp.concatenate([left[n, pl.ds(c + k, 64, stride=32), :] for n in range(2)], axis=1)
                for k in range(2)
            ],
            axis=0,
        )
        product = (dot_nt(rows.astype(BF16), right) * (1.0 / 256)).astype(BF16)
        for k in range(2):
            for g in range(8):
                wide[g * 64 : g * 64 + 64, (c + k) * 128 : (c + k) * 128 + 128] = product[
                    k * 64 : k * 64 + 64, g * 128 : g * 128 + 128
                ]
    update = dot(wide[...], block[...])
    for g in range(8):
        for j in range(4):
            pairs[pl.ds(g * 4 + j, 64, stride=32), :] = update[g * 64 : g * 64 + 64, j * 128 : j * 128 + 128]
    out_ref[...] = pairs[...].astype(BF16)


def whole_kernel(
    x_hbm, pair_hbm, bw_hbm, rw_hbm, ro_hbm, cw_hbm, co_hbm, ti_hbm, to_hbm, oi_hbm, oo_hbm,
    ao_hbm, pu_hbm,
    pair, bw, rw, ro, cw, co, ti, to, oi, oo,
    own, xo, bias, qd, kk, vt, gt, mask, mid, mix, wt, sendbuf, cells, ot, fl, fr, lo, ri, left, wide, block, pairs,
    ao, pu,
    send, recv, ssend, srecv, xsend, xrecv, csend, crecv, lsend, lrecv, rsend, rrecv, lsem,
):
    s, r = lax.axis_index("seq"), lax.axis_index("res")
    here = s * RES + r
    pos = {"x": s // 2, "y": (s % 2) * 2 + r // 8, "z": (r % 8) // 2}
    core = r % 2
    sibling = (s, r + 1 - 2 * core)

    def near(dim, by):
        at = dict(pos)
        at[dim] = (pos[dim] + by) % 4
        return device(at["x"], at["y"], at["z"], core)

    loads = {}
    for k, (name, src, dst) in enumerate(
        (
            ("pair", pair_hbm, pair), ("bw", bw_hbm, bw), ("rw", rw_hbm, rw), ("ro", ro_hbm, ro), ("cw", cw_hbm, cw),
            ("co", co_hbm, co), ("ti", ti_hbm, ti), ("to", to_hbm, to), ("oi", oi_hbm, oi), ("oo", oo_hbm, oo),
            ("keep", x_hbm.at[r], xo.at[r]),
        )
    ):
        loads[name] = pltpu.make_async_copy(src, dst, lsem.at[k])
        loads[name].start()
    barrier = pltpu.get_barrier_semaphore()

    def greet(k, carry):
        other = (here + k) % 128
        pl.semaphore_signal(barrier, inc=1, device_id=(other // RES, other % RES), device_id_type=MESH)
        return carry

    lax.fori_loop(1, 128, greet, 0)

    loads["pair"].wait()
    loads["bw"].wait()
    pair_bias(pair, bw, own)
    mine_at = bias.at[:, pos["x"], pos["y"], pos["z"], core]
    place = pltpu.make_async_copy(own, mine_at, lsem.at[0])
    place.start()
    pl.semaphore_wait(barrier, 127)

    def box(t, known, dim, at, rows):
        index = [t]
        for d in "xyz":
            index.append(pl.ds(0, 4) if d in known else (at if d == dim else pos[d]))
        return bias.at[(*index, core, rows)]

    everything = pl.ds(0, 32)
    started = []

    def ring(t, phase, k, src, dst, target):
        copy = remote(src, dst, send.at[t, phase, k], recv.at[t, phase, k], target)
        copy.start()
        started.append(copy)
        return copy

    def share(t, k, src, dst):
        copy = remote(src, dst, ssend.at[t, k], srecv, sibling)
        copy.start()
        started.append(copy)

    def between(phase, half):
        if phase == 0 and half == 0:
            row = lax.broadcasted_iota(jnp.int32, (C, 512), 0) // D
            lane = lax.broadcasted_iota(jnp.int32, (C, 512), 1) // 64
            mask[...] = jnp.where(row == lane, 1.0, 0.0).astype(BF16)
            loads["rw"].wait()
            loads["cw"].wait()
            for k, w in enumerate((rw, cw)):
                for i, at in enumerate((0, 2, 3)):
                    wt[k, i * C : i * C + C, :] = w[:, at * C : at * C + C].T
        if phase == 0 and half == 1:
            loads["oo"].wait()
            outer_weight(oo, block)
        if phase == 1 and half == 1:
            loads["keep"].wait()
            most = xo.at[pl.ds(0, 15)]
            remote(most, most, xsend, xrecv, sibling).wait()
        if phase == 2:
            row_project(half, xo, wt.at[0], rw[:, C : 2 * C], qd, kk, vt, gt)

    for phase in range(3):
        first = {}
        for t in range(4):
            dim, known = ORDERS[t][phase], ORDERS[t][:phase]
            mine = box(t, known, dim, pos[dim], everything)
            src = own.at[t] if phase == 0 else mine
            for k, by in enumerate((1, 3)):
                first[t, k] = ring(t, phase, k, src, mine, near(dim, by))
            if phase == 0:
                share(t, 0, src, mine)
        if phase == 0:

            def scatter(k, carry):
                other = (r + k) % 16
                remote(x_hbm.at[other], xo.at[r], xsend, xrecv, (s, other)).start()
                return carry

            lax.fori_loop(1, 16, scatter, 0)
        between(phase, 0)
        second = {}
        for t in range(4):
            dim, known = ORDERS[t][phase], ORDERS[t][:phase]
            for k, by in enumerate((1, 3)):
                first[t, k].wait_recv()
                at = (pos[dim] + (3, 1)[k]) % 4
                part = box(t, known, dim, at, pl.ds(16 * k, 16))
                second[t, k] = ring(t, phase, 2 + k, part, part, near(dim, by))
                all_of = box(t, known, dim, at, everything)
                share(t, 1 + phase * 4 + k, all_of, all_of)
        between(phase, 1)
        for t in range(4):
            dim, known = ORDERS[t][phase], ORDERS[t][:phase]
            for k in range(2):
                second[t, k].wait_recv()
                part = box(t, known, dim, (pos[dim] + 2) % 4, pl.ds(16 * k, 16))
                share(t, 3 + phase * 4 + k, part, part)
        if phase == 0:
            place.wait()
    half = bias.at[:, :, :, :, 0]
    remote(half, half, lsem.at[0], srecv, sibling).wait_recv()

    loads["ro"].wait()

    def quarter(k, carry):
        sp = (pos["x"] + k) % 4

        def one(n, carry):
            row_attend(n, sp, xo, bias, ro, qd, kk, vt, gt, mask, mid, mix)
            return carry

        lax.fori_loop(0, 2, one, 0)
        rows = mix[pl.ds(pl.multiple_of(sp * 512, 512), 512), :].astype(BF16)
        sendbuf[pl.ds(sp * 32, 32)] = rows.reshape(32, 16, 128)

        def scatter(i, carry):
            other = sp * 32 + (here + i) % 32

            @pl.when(other != here)
            def _():
                remote(sendbuf.at[other], cells.at[here], csend, crecv, (other // RES, other % RES)).start()

            return carry

        lax.fori_loop(0, 32, scatter, 0)
        return carry

    lax.fori_loop(0, 4, quarter, 0)
    cells[here] = sendbuf[here]
    for copy in started:
        copy.wait_send()
    for name in ("cw", "co", "ti", "to", "oi"):
        if name != "cw":
            loads[name].wait()
    most = cells.at[pl.ds(0, 127)]
    remote(most, most, csend, crecv, sibling).wait()

    mix[...] = cells[...].reshape(2048, 128).astype(F32)
    wf = oi[...].T
    column = 2 * s + r // 8
    is_own = column == r

    def residue(a, carry):
        factor = column_step(a, mix, wt.at[1], cw[:, C : 2 * C], co, ti, to, wf, ot)
        fl[a] = factor[:D]
        fr[a] = factor[D:]
        lo[r, a] = factor[:D]

        @pl.when(is_own)
        def _():
            ri[r % 8, a] = factor[D:]

        def send_left(k, carry):
            remote(fl.at[a], lo.at[r, a], lsend, lrecv, (s, (r + k) % 16)).start()
            return carry

        def send_right(k, carry):
            @pl.when(jnp.logical_not(jnp.logical_and(is_own, k == 0)))
            def _():
                remote(fr.at[a], ri.at[r % 8, a], rsend, rrecv, ((s + k) % 8, column)).start()

            return carry

        lax.fori_loop(1, 16, send_left, 0)
        lax.fori_loop(0, 8, send_right, 0)
        return carry

    lax.fori_loop(0, 4, residue, 0)
    ao[...] = mix[...].astype(BF16)
    save = pltpu.make_async_copy(ao, ao_hbm, lsem.at[0])
    save.start()
    most = lo.at[pl.ds(0, 15)]
    remote(most, most, lsend, lrecv, sibling).wait()

    @pl.when(is_own)
    def _():
        part = ri.at[pl.ds(0, 7)]
        remote(part, part, rsend, rrecv, sibling).wait()

    @pl.when(jnp.logical_not(is_own))
    def _():
        remote(ri, ri, rsend, rrecv, sibling).wait()

    outer_part(lo, ri, pu, left, wide, block, pairs)
    last = pltpu.make_async_copy(pu, pu_hbm, lsem.at[1])
    last.start()
    last.wait()
    save.wait()


def body(
    alignment,
    pair_state,
    bias_weight,
    row_weight,
    row_output_weight,
    column_weight,
    column_output_weight,
    transition_in,
    transition_out,
    outer_in,
    outer_out,
):
    dma = pltpu.SemaphoreType.DMA
    new, update = pl.pallas_call(
        whole_kernel,
        out_shape=(jax.ShapeDtypeStruct((2048, 128), BF16), jax.ShapeDtypeStruct((2048, 128), BF16)),
        in_specs=[ANY] * 11,
        out_specs=(ANY, ANY),
        scratch_shapes=[
            pltpu.VMEM((64, 32, 128), BF16),
            pltpu.VMEM((128, 8), BF16),
            pltpu.VMEM((C, 4 * C), BF16),
            pltpu.VMEM((C, C), BF16),
            pltpu.VMEM((C, 4 * C), BF16),
            pltpu.VMEM((C, C), BF16),
            pltpu.VMEM((C, 4 * C), BF16),
            pltpu.VMEM((4 * C, C), BF16),
            pltpu.VMEM((C, 64), BF16),
            pltpu.VMEM((1024, 128), BF16),
            pltpu.VMEM((4, 32, 128), BF16),
            pltpu.VMEM((16, 2, 32, C), BF16),
            pltpu.VMEM((4, 4, 4, 4, 2, 32, 128), BF16),
            pltpu.VMEM((2, 8, C, 128), BF16),
            pltpu.VMEM((2, 512, C), BF16),
            pltpu.VMEM((2, C, 512), BF16),
            pltpu.VMEM((2, 4, C, 128), BF16),
            pltpu.VMEM((C, 512), BF16),
            pltpu.VMEM((2, 128, 128), F32),
            pltpu.VMEM((2048, 128), F32),
            pltpu.VMEM((2, 3 * C, C), BF16),
            pltpu.VMEM((128, 16, 128), BF16),
            pltpu.VMEM((128, 16, 128), BF16),
            pltpu.VMEM((C, 256), F32),
            pltpu.VMEM((4, D, 256), BF16),
            pltpu.VMEM((4, D, 256), BF16),
            pltpu.VMEM((16, 4, D, 256), BF16),
            pltpu.VMEM((8, 4, D, 256), BF16),
            pltpu.VMEM((2, 2048, 128), F32),
            pltpu.VMEM((512, 4096), BF16),
            pltpu.VMEM((4096, 512), BF16),
            pltpu.VMEM((2048, 128), F32),
            pltpu.VMEM((2048, 128), BF16),
            pltpu.VMEM((2048, 128), BF16),
            dma((4, 3, 4)),
            dma((4, 3, 4)),
            dma((4, 13)),
        ]
        + [dma] * 9
        + [dma((11,))],
        compiler_params=pltpu.CompilerParams(collective_id=0, has_side_effects=True, vmem_limit_bytes=56 << 20),
        name="evoformer",
    )(
        alignment.reshape(16, 2, 32, C),
        pair_state,
        bias_weight,
        row_weight,
        row_output_weight,
        column_weight,
        column_output_weight,
        transition_in,
        transition_out,
        outer_in,
        outer_out,
    )
    pair_update = update.reshape(64, 32, 128)
    alignment_out = new.reshape(128, 2, 2, 4, 128).transpose(0, 1, 3, 2, 4).reshape(256, 4, C)
    return (alignment_out, pair_update)


def solution(mesh):
    in_specs = (P("seq", "res", None), P("seq", "res", None)) + (P(),) * 9
    out_specs = (P(None, ("seq", "res"), None), P("seq", "res", None))
    return jax.shard_map(body, mesh=mesh, in_specs=in_specs, out_specs=out_specs, check_vma=False)
```

time: 363 us -> 99.6 us (0.27); the launches traced: 358 us -> 99.4 us
  waiting for transfers between devices: 144 us -> 0 us
  Pallas kernels: 0 us -> 93.7 us
  local copies, waits for them, and re-layouts: 65.3 us -> 5.01 us
  matrix products: 56.3 us -> 0 us
  blocking collectives: 53.8 us -> 0 us
  between operations: 14.2 us -> 0.66 us
  starting transfers between devices: 12.5 us -> 0 us
  other arithmetic: 11.7 us -> 0 us
    pallas_call x0 -> x1, Pallas kernels: none -> 93.7 us  [body(): pl.pallas_call(whole_kernel, out_shape=(jax.ShapeDtypeStruct((2048, 128),...]
    psum x1 -> x0, waiting for transfers between devices: 82.5 us -> none  [from_root(): return lax.psum(kept, axis)]
    all_gather x2 -> x0, waiting for transfers between devices: 50.5 us -> none  [the longest x1 30.8 us: body(): row_side = lax.all_gather(factors, 'res', axis=1, tiled=True)]
    dot_general x14 -> x0, matrix products: 44.9 us -> none  [the longest x2 13.6 us: body(): jnp.einsum('sic,sjd->ijcd', left_block, right_cols, preferred_element_typ...]
    all_gather x1 -> x0, blocking collectives: 32.7 us -> none  [body(): column_bias = lax.all_gather(tile_bias, 'seq', axis=1, tiled=True)]
    convert_element_type x7 -> x0, local copies, waits for them, and re-layouts: 25.4 us -> none  [the longest x2 24 us: body(): outer_sum.astype(jnp.bfloat16)]
    reshape x3 -> x0, local copies, waits for them, and re-layouts: 25.1 us -> none  [the longest x2 23.8 us: body(): outer_sum.astype(jnp.bfloat16)]
    all_to_all x1 -> x0, blocking collectives: 21.1 us -> none  [body(): lax.all_to_all(row_alignment_state, ('seq', 'res'), split_axis=1, concat_...]
  transfers between devices with their start and end apart: 4 -> 0, of which waited for: 4 -> 0; matrix products, arithmetic and copies ran while one was open for 1% -> 0% of each run, Pallas kernels for 0% -> 0%
where the time goes in v2:
time: 99.6 us; the launch traced here: 99.4 us
  Pallas kernels  93.7 us (94%)
  local copies, waits for them, and re-layouts  5.01 us (5%)
    pallas_call x1, Pallas kernels, body(): pl.pallas_call(whole_kernel, out_shape=(jax.ShapeDtypeStruct((2048, 128),...  93.7 us
    unnamed x8, local copies, waits for them, and re-layouts  5.01 us

profile of v2, /device:TPU:1, one launch (start us, length us, event | category | flops | bytes accessed | tf_op | source)
XLA Modules:
  0.0 99.4 jit_solution(5320035505912866870)
XLA Ops:
  0.6 0.0 copy-start.1
  0.6 1.4 %copy.13.bw_hbm = bf16[128,8]{1,0:T(8,128)(2,1)} copy(bf16[128,8]{0,1:T(8,128)(2,1)} %param.13) | data formatting | bytes 4096 | tf_op args[2]
  2.0 0.0 copy-done.1
  2.0 0.7 copy.14.oi_hbm
  2.8 93.7 %evoformer.1 = (bf16[2048,128]{1,0:T(8,128)(2,1)}, bf16[2048,128]{1,0:T(8,128)(2,1)}) custom-call(bf16[16,2,32,256]{3,2,1,0:T(8,128)(2,1)} %bitcast.7, bf16[64,32,128]{2,1,0:T(8,128)(2,1)} %pair_hbm.1, bf16[128,8]{1,0:T(8,128)(2,1)} %copy.13.bw_hbm, bf16[256,1024]{1,0:T(8,128)(2,1)} %rw_hbm.1, bf16[256,256]{1,0:T(8,128)(2,1)} %ro_hbm.1, ...), custom_call_target="tpu_custom_call" | custom-call | tf_op jit(solution)/shard_map/evoformer/pallas_call | solution.py:424
  96.5 0.0 copy-start
  96.5 2.1 %copy.18 = bf16[256,4,256]{2,1,0:T(4,128)(2,1)} copy(bf16[256,4,256]{2,1,0:T(4,128)(2,1)} %bitcast.9) | data formatting | bytes 1048576
  98.6 0.0 copy-done
  98.6 0.8 copy.19
Async XLA Ops:
  0.6 1.4 %copy-start.1 = (bf16[256,64]{0,1:T(8,128)(2,1)S(1)}, bf16[256,64]{0,1:T(8,128)(2,1)}, u32[]{:S(2)}) copy-start(bf16[256,64]{0,1:T(8,128)(2,1)} %param.20) | copy-start | bytes 98308
  96.5 2.1 %copy-start = (bf16[2048,128]{1,0:T(8,128)(2,1)S(1)}, bf16[2048,128]{1,0:T(8,128)(2,1)}, u32[]{:S(2)}) copy-start(bf16[2048,128]{1,0:T(8,128)(2,1)} %get-tuple-element.5) | copy-start | bytes 1572868

commit v3 on v2

--- a/solution.py
+++ b/solution.py
@@ -59,20 +59,14 @@
     )
 
 
-ORDERS = ("zyx", "xzy", "yxz", "zyx")
-
-
 def pair_bias(pair_ref, weight_ref, out_ref):
     lane = lax.broadcasted_iota(jnp.int32, (32, 512), 1) % 64
-    low = lax.broadcasted_iota(jnp.int32, (128, 128), 1) < 64
     narrow = weight_ref[...].astype(F32)
-    weight = jnp.concatenate(
-        [jnp.where(low, narrow[:, 2 * t : 2 * t + 1], narrow[:, 2 * t + 1 : 2 * t + 2]) for t in range(4)], axis=1
-    ).astype(BF16)
+    weight = jnp.concatenate([jnp.broadcast_to(narrow[h : h + 1], (64, 128)) for h in range(8)], axis=0).astype(BF16)
 
     def step(k, total):
         rows = pair_ref[pl.ds(k * 8, 8)].reshape(256, 128).astype(F32)
-        spread = dot(layer_norm(rows).astype(BF16), weight)
+        spread = dot_nt(layer_norm(rows).astype(BF16), weight)
         for one in range(8):
             total = jnp.where(lane == k * 8 + one, spread[one * 32 : one * 32 + 32], total)
         return total
@@ -156,7 +150,7 @@
             mix[pl.ds(n * 8 + ch * 4 + a, 128, stride=16), :] = new[
                 n * 128 : n * 128 + 128, ch * 128 : ch * 128 + 128
             ]
-    return dot_nt(wf[...], layer_norm(new).astype(BF16)).astype(BF16)
+    return dot_nt(wf, layer_norm(new).astype(BF16)).astype(BF16)
 
 
 def outer_weight(w_ref, block):
@@ -169,7 +163,7 @@
 
 def outer_part(left_ref, right_ref, out_ref, left, wide, block, pairs):
     for n in range(2):
-        left[n] = left_ref[:, :, :, n * 128 : n * 128 + 128].reshape(2048, 128).astype(F32)
+        left[n] = left_ref[:, :, :, :, n * 128 : n * 128 + 128].reshape(2048, 128).astype(F32)
     right = right_ref[...].reshape(1024, 256)
     for c in range(0, 32, 2):
         rows = jnp.concatenate(
@@ -198,7 +192,8 @@
     pair, bw, rw, ro, cw, co, ti, to, oi, oo,
     own, xo, bias, qd, kk, vt, gt, mask, mid, mix, wt, sendbuf, cells, ot, fl, fr, lo, ri, left, wide, block, pairs,
     ao, pu,
-    send, recv, ssend, srecv, xsend, xrecv, csend, crecv, lsend, lrecv, rsend, rrecv, lsem,
+    zsend, zrecv, ysend, yrecv, hrecv, srecv, lrecv, lsem,
+    hsend, ssend, xsend, xrecv, csend, crecv, lsend, fsend, frecv, rsend, rrecv,
 ):
     s, r = lax.axis_index("seq"), lax.axis_index("res")
     here = s * RES + r
@@ -221,6 +216,10 @@
     ):
         loads[name] = pltpu.make_async_copy(src, dst, lsem.at[k])
         loads[name].start()
+
+    def need(name):
+        loads.pop(name).wait()
+
     barrier = pltpu.get_barrier_semaphore()
 
     def greet(k, carry):
@@ -230,147 +229,194 @@
 
     lax.fori_loop(1, 128, greet, 0)
 
-    loads["pair"].wait()
-    loads["bw"].wait()
+    need("pair")
+    need("bw")
     pair_bias(pair, bw, own)
     mine_at = bias.at[:, pos["x"], pos["y"], pos["z"], core]
     place = pltpu.make_async_copy(own, mine_at, lsem.at[0])
     place.start()
     pl.semaphore_wait(barrier, 127)
 
-    def box(t, known, dim, at, rows):
-        index = [t]
-        for d in "xyz":
-            index.append(pl.ds(0, 4) if d in known else (at if d == dim else pos[d]))
-        return bias.at[(*index, core, rows)]
-
-    everything = pl.ds(0, 32)
-    started = []
-
-    def ring(t, phase, k, src, dst, target):
-        copy = remote(src, dst, send.at[t, phase, k], recv.at[t, phase, k], target)
+    def scatter_x(k, carry):
+        other = (r + k) % 16
+        remote(x_hbm.at[other], xo.at[r], xsend, xrecv, (s, other)).start()
+        return carry
+
+    def line(x, y, ts=pl.ds(0, 4)):
+        return bias.at[ts, x, y, :, core]
+
+    def share(plane, what):
+        remote(what, what, ssend, srecv.at[plane], sibling).start()
+
+    parts = (pl.ds(0, 2), pl.ds(2, 2))
+    px, py, pz = pos["x"], pos["y"], pos["z"]
+
+    def along_x(k, y):
+        for way, by in enumerate((1, 3)):
+            remote(line(px, y), line(px, y), hsend, hrecv.at[k, way], near("x", by)).start()
+
+    def onward_x(k, y):
+        for way, by in enumerate((1, 3)):
+            x = (px + (3, 1)[way]) % 4
+            remote(line(x, y), line(x, y), hsend, hrecv.at[k, way], near("x", by)).wait_recv()
+            part = line(x, y, parts[way])
+            remote(part, part, hsend, hrecv.at[k, 2 + way], near("x", by)).start()
+            share(1 + way, line(x, y))
+
+    def last_x(k, y):
+        for way, by in enumerate((1, 3)):
+            part = line((px + 2) % 4, y, parts[way])
+            remote(part, part, hsend, hrecv.at[k, 2 + way], near("x", by)).wait_recv()
+        share(3, line((px + 2) % 4, y))
+
+    def shared(plane, x):
+        half = bias.at[:, x, :, :, 1 - core]
+        remote(half, half, hsend, srecv.at[plane], sibling).wait_recv()
+
+    first_z = [
+        remote(own, bias.at[:, px, py, pz, core], zsend.at[k], zrecv.at[k], near("z", by)) for k, by in enumerate((1, 3, 2))
+    ]
+    for copy in first_z:
         copy.start()
-        started.append(copy)
-        return copy
-
-    def share(t, k, src, dst):
-        copy = remote(src, dst, ssend.at[t, k], srecv, sibling)
+    lax.fori_loop(1, 16, scatter_x, 0)
+
+    row = lax.broadcasted_iota(jnp.int32, (C, 512), 0) // D
+    lane = lax.broadcasted_iota(jnp.int32, (C, 512), 1) // 64
+    mask[...] = jnp.where(row == lane, 1.0, 0.0).astype(BF16)
+    need("rw")
+    for i, at in enumerate((0, 2, 3)):
+        wt[0, i * C : i * C + C, :] = rw[:, at * C : at * C + C].T
+
+    place.wait()
+    for copy in first_z:
+        copy.wait_recv()
+    first_y = [
+        remote(line(px, py), line(px, py), ysend.at[k], yrecv.at[k], near("y", by)) for k, by in enumerate((1, 3))
+    ]
+    for copy in first_y:
         copy.start()
-        started.append(copy)
-
-    def between(phase, half):
-        if phase == 0 and half == 0:
-            row = lax.broadcasted_iota(jnp.int32, (C, 512), 0) // D
-            lane = lax.broadcasted_iota(jnp.int32, (C, 512), 1) // 64
-            mask[...] = jnp.where(row == lane, 1.0, 0.0).astype(BF16)
-            loads["rw"].wait()
-            loads["cw"].wait()
-            for k, w in enumerate((rw, cw)):
-                for i, at in enumerate((0, 2, 3)):
-                    wt[k, i * C : i * C + C, :] = w[:, at * C : at * C + C].T
-        if phase == 0 and half == 1:
-            loads["oo"].wait()
-            outer_weight(oo, block)
-        if phase == 1 and half == 1:
-            loads["keep"].wait()
-            most = xo.at[pl.ds(0, 15)]
-            remote(most, most, xsend, xrecv, sibling).wait()
-        if phase == 2:
-            row_project(half, xo, wt.at[0], rw[:, C : 2 * C], qd, kk, vt, gt)
-
-    for phase in range(3):
-        first = {}
-        for t in range(4):
-            dim, known = ORDERS[t][phase], ORDERS[t][:phase]
-            mine = box(t, known, dim, pos[dim], everything)
-            src = own.at[t] if phase == 0 else mine
-            for k, by in enumerate((1, 3)):
-                first[t, k] = ring(t, phase, k, src, mine, near(dim, by))
-            if phase == 0:
-                share(t, 0, src, mine)
-        if phase == 0:
-
-            def scatter(k, carry):
-                other = (r + k) % 16
-                remote(x_hbm.at[other], xo.at[r], xsend, xrecv, (s, other)).start()
+    along_x(0, py)
+    share(0, line(px, py))
+    need("cw")
+    for i, at in enumerate((0, 2, 3)):
+        wt[1, i * C : i * C + C, :] = cw[:, at * C : at * C + C].T
+    second_y = []
+    for k, by in enumerate((1, 3)):
+        first_y[k].wait_recv()
+        y = (py + (3, 1)[k]) % 4
+        part = line(px, y, parts[k])
+        second_y.append(remote(part, part, ysend.at[2 + k], yrecv.at[2 + k], near("y", by)))
+        second_y[k].start()
+        along_x(1 + k, y)
+        share(0, line(px, y))
+    need("oo")
+    outer_weight(oo, block)
+    for copy in second_y:
+        copy.wait_recv()
+    along_x(3, (py + 2) % 4)
+    share(0, line(px, (py + 2) % 4))
+    need("keep")
+    most = xo.at[pl.ds(0, 15)]
+    remote(most, most, xsend, xrecv, sibling).wait()
+    row_project(0, xo, wt.at[0], rw[:, C : 2 * C], qd, kk, vt, gt)
+    onward_x(0, py)
+    row_project(1, xo, wt.at[0], rw[:, C : 2 * C], qd, kk, vt, gt)
+    onward_x(1, (py + 3) % 4)
+    need("ro")
+
+    def attend(index, carry):
+        q = index // 2
+        n = index % 2
+        sp = (px + q - q // 2 + 2 * (q % 2) * (1 - q // 2)) % 4
+
+        @pl.when(index == 0)
+        def _():
+            shared(0, px)
+
+        @pl.when(index == 1)
+        def _():
+            onward_x(2, (py + 1) % 4)
+
+        @pl.when(index == 2)
+        def _():
+            onward_x(3, (py + 2) % 4)
+            shared(1, (px + 3) % 4)
+
+        @pl.when(index == 3)
+        def _():
+            last_x(0, py)
+
+        @pl.when(index == 4)
+        def _():
+            shared(2, (px + 1) % 4)
+
+        @pl.when(index == 5)
+        def _():
+            last_x(1, (py + 3) % 4)
+
+        @pl.when(index == 6)
+        def _():
+            last_x(2, (py + 1) % 4)
+            last_x(3, (py + 2) % 4)
+            shared(3, (px + 2) % 4)
+
+        row_attend(n, sp, xo, bias, ro, qd, kk, vt, gt, mask, mid, mix)
+
+        @pl.when(n == 1)
+        def _():
+            rows = mix[pl.ds(pl.multiple_of(sp * 512, 512), 512), :].astype(BF16)
+            sendbuf[pl.ds(sp * 32, 32)] = rows.reshape(32, 16, 128)
+
+            def scatter(i, carry):
+                other = sp * 32 + (here + i) % 32
+
+                @pl.when(other != here)
+                def _():
+                    remote(sendbuf.at[other], cells.at[here], csend, crecv, (other // RES, other % RES)).start()
+
                 return carry
 
-            lax.fori_loop(1, 16, scatter, 0)
-        between(phase, 0)
-        second = {}
-        for t in range(4):
-            dim, known = ORDERS[t][phase], ORDERS[t][:phase]
-            for k, by in enumerate((1, 3)):
-                first[t, k].wait_recv()
-                at = (pos[dim] + (3, 1)[k]) % 4
-                part = box(t, known, dim, at, pl.ds(16 * k, 16))
-                second[t, k] = ring(t, phase, 2 + k, part, part, near(dim, by))
-                all_of = box(t, known, dim, at, everything)
-                share(t, 1 + phase * 4 + k, all_of, all_of)
-        between(phase, 1)
-        for t in range(4):
-            dim, known = ORDERS[t][phase], ORDERS[t][:phase]
-            for k in range(2):
-                second[t, k].wait_recv()
-                part = box(t, known, dim, (pos[dim] + 2) % 4, pl.ds(16 * k, 16))
-                share(t, 3 + phase * 4 + k, part, part)
-        if phase == 0:
-            place.wait()
-    half = bias.at[:, :, :, :, 0]
-    remote(half, half, lsem.at[0], srecv, sibling).wait_recv()
-
-    loads["ro"].wait()
-
-    def quarter(k, carry):
-        sp = (pos["x"] + k) % 4
-
-        def one(n, carry):
-            row_attend(n, sp, xo, bias, ro, qd, kk, vt, gt, mask, mid, mix)
-            return carry
-
-        lax.fori_loop(0, 2, one, 0)
-        rows = mix[pl.ds(pl.multiple_of(sp * 512, 512), 512), :].astype(BF16)
-        sendbuf[pl.ds(sp * 32, 32)] = rows.reshape(32, 16, 128)
-
-        def scatter(i, carry):
-            other = sp * 32 + (here + i) % 32
-
-            @pl.when(other != here)
-            def _():
-                remote(sendbuf.at[other], cells.at[here], csend, crecv, (other // RES, other % RES)).start()
-
-            return carry
-
-        lax.fori_loop(0, 32, scatter, 0)
+            lax.fori_loop(0, 32, scatter, 0)
+
         return carry
 
-    lax.fori_loop(0, 4, quarter, 0)
+    lax.fori_loop(0, 8, attend, 0)
     cells[here] = sendbuf[here]
-    for copy in started:
+    for copy in first_z + first_y + second_y:
         copy.wait_send()
-    for name in ("cw", "co", "ti", "to", "oi"):
-        if name != "cw":
-            loads[name].wait()
+    most = bias.at[:, :, :, :, 0]
+    remote(most, most, ssend, srecv.at[0], sibling).wait_send()
+    most = bias.at[:, pl.ds(0, 3), :, :, 0]
+    remote(most, most, hsend, srecv.at[0], sibling).wait_send()
+    for name in ("co", "ti", "to", "oi"):
+        need(name)
     most = cells.at[pl.ds(0, 127)]
     remote(most, most, csend, crecv, sibling).wait()
 
     mix[...] = cells[...].reshape(2048, 128).astype(F32)
-    wf = oi[...].T
+    wf = oi[...]
     column = 2 * s + r // 8
     is_own = column == r
+    chip = r // 2
+
+    def onward_left(a):
+        most = lo.at[pl.ds(0, 7), core, a]
+        remote(most, most, lsend, lrecv.at[a], sibling).wait_recv()
+        line = lo.at[:, core, a]
+        remote(line, line, fsend, frecv, sibling).start()
 
     def residue(a, carry):
         factor = column_step(a, mix, wt.at[1], cw[:, C : 2 * C], co, ti, to, wf, ot)
         fl[a] = factor[:D]
         fr[a] = factor[D:]
-        lo[r, a] = factor[:D]
+        lo[chip, core, a] = factor[:D]
 
         @pl.when(is_own)
         def _():
             ri[r % 8, a] = factor[D:]
 
         def send_left(k, carry):
-            remote(fl.at[a], lo.at[r, a], lsend, lrecv, (s, (r + k) % 16)).start()
+            remote(fl.at[a], lo.at[chip, core, a], lsend, lrecv.at[a], (s, ((chip + k) % 8) * 2 + core)).start()
             return carry
 
         def send_right(k, carry):
@@ -380,16 +426,24 @@
 
             return carry
 
-        lax.fori_loop(1, 16, send_left, 0)
+        lax.fori_loop(1, 8, send_left, 0)
         lax.fori_loop(0, 8, send_right, 0)
+
+        @pl.when(a > 0)
+        def _():
+            onward_left(a - 1)
+
         return carry
 
     lax.fori_loop(0, 4, residue, 0)
     ao[...] = mix[...].astype(BF16)
     save = pltpu.make_async_copy(ao, ao_hbm, lsem.at[0])
     save.start()
-    most = lo.at[pl.ds(0, 15)]
-    remote(most, most, lsend, lrecv, sibling).wait()
+    onward_left(3)
+    most = lo.at[pl.ds(0, 7), core]
+    remote(most, most, lsend, frecv, sibling).wait_send()
+    half = lo.at[:, 1 - core]
+    remote(half, half, fsend, frecv, sibling).wait()
 
     @pl.when(is_own)
     def _():
@@ -428,14 +482,14 @@
         out_specs=(ANY, ANY),
         scratch_shapes=[
             pltpu.VMEM((64, 32, 128), BF16),
-            pltpu.VMEM((128, 8), BF16),
+            pltpu.VMEM((8, 128), BF16),
             pltpu.VMEM((C, 4 * C), BF16),
             pltpu.VMEM((C, C), BF16),
             pltpu.VMEM((C, 4 * C), BF16),
             pltpu.VMEM((C, C), BF16),
             pltpu.VMEM((C, 4 * C), BF16),
             pltpu.VMEM((4 * C, C), BF16),
-            pltpu.VMEM((C, 64), BF16),
+            pltpu.VMEM((64, C), BF16),
             pltpu.VMEM((1024, 128), BF16),
             pltpu.VMEM((4, 32, 128), BF16),
             pltpu.VMEM((16, 2, 32, C), BF16),
@@ -453,7 +507,7 @@
             pltpu.VMEM((C, 256), F32),
             pltpu.VMEM((4, D, 256), BF16),
             pltpu.VMEM((4, D, 256), BF16),
-            pltpu.VMEM((16, 4, D, 256), BF16),
+            pltpu.VMEM((8, 2, 4, D, 256), BF16),
             pltpu.VMEM((8, 4, D, 256), BF16),
             pltpu.VMEM((2, 2048, 128), F32),
             pltpu.VMEM((512, 4096), BF16),
@@ -461,25 +515,29 @@
             pltpu.VMEM((2048, 128), F32),
             pltpu.VMEM((2048, 128), BF16),
             pltpu.VMEM((2048, 128), BF16),
-            dma((4, 3, 4)),
-            dma((4, 3, 4)),
-            dma((4, 13)),
+            dma((3,)),
+            dma((3,)),
+            dma((4,)),
+            dma((4,)),
+            dma((4, 4)),
+            dma((4,)),
+            dma((4,)),
+            dma((11,)),
         ]
-        + [dma] * 9
-        + [dma((11,))],
+        + [dma] * 11,
         compiler_params=pltpu.CompilerParams(collective_id=0, has_side_effects=True, vmem_limit_bytes=56 << 20),
         name="evoformer",
     )(
         alignment.reshape(16, 2, 32, C),
         pair_state,
-        bias_weight,
+        bias_weight.T,
         row_weight,
         row_output_weight,
         column_weight,
         column_output_weight,
         transition_in,
         transition_out,
-        outer_in,
+        outer_in.T,
         outer_out,
     )
     pair_update = update.reshape(64, 32, 128)

time: 99.6 us -> 89.9 us (0.903)
  Pallas kernels: 93.7 us -> 86.3 us
  local copies, waits for them, and re-layouts: 5.01 us -> 2.87 us
    pallas_call x1, Pallas kernels: 93.7 us -> 86.3 us  [body(): pl.pallas_call(whole_kernel, out_shape=(jax.ShapeDtypeStruct((2048, 128),...]
    unnamed x8 -> x4, local copies, waits for them, and re-layouts: 5.01 us -> 2.87 us
where the time goes in v3:
time: 89.9 us; the launch traced here: 89.8 us
  Pallas kernels  86.3 us (96%)
  local copies, waits for them, and re-layouts  2.87 us (3%)
    pallas_call x1, Pallas kernels, body(): pl.pallas_call(whole_kernel, out_shape=(jax.ShapeDtypeStruct((2048, 128),...  86.3 us
    unnamed x4, local copies, waits for them, and re-layouts  2.87 us

profile of v3, /device:TPU:1, one launch (start us, length us, event | category | flops | bytes accessed | tf_op | source)
XLA Modules:
  0.0 89.8 jit_solution(16428597742522362578)
XLA Ops:
  0.6 86.3 %evoformer.1 = (bf16[2048,128]{1,0:T(8,128)(2,1)}, bf16[2048,128]{1,0:T(8,128)(2,1)}) custom-call(bf16[16,2,32,256]{3,2,1,0:T(8,128)(2,1)} %bitcast.9, bf16[64,32,128]{2,1,0:T(8,128)(2,1)} %pair_hbm.1, bf16[8,128]{1,0:T(8,128)(2,1)} %bitcast.13, bf16[256,1024]{1,0:T(8,128)(2,1)} %rw_hbm.1, bf16[256,256]{1,0:T(8,128)(2,1)} %ro_hbm.1, ...), custom_call_target="tpu_custom_call" | custom-call | tf_op jit(solution)/shard_map/evoformer/pallas_call | solution.py:478
  86.9 0.0 copy-start
  86.9 2.1 %copy.16 = bf16[256,4,256]{2,1,0:T(4,128)(2,1)} copy(bf16[256,4,256]{2,1,0:T(4,128)(2,1)} %bitcast.11) | data formatting | bytes 1048576
  89.0 0.0 copy-done
  89.0 0.8 copy.17
Async XLA Ops:
  86.9 2.1 %copy-start = (bf16[2048,128]{1,0:T(8,128)(2,1)S(1)}, bf16[2048,128]{1,0:T(8,128)(2,1)}, u32[]{:S(2)}) copy-start(bf16[2048,128]{1,0:T(8,128)(2,1)} %get-tuple-element.5) | copy-start | bytes 1572868

commit v4 on v3

--- a/solution.py
+++ b/solution.py
@@ -90,40 +90,42 @@
         qd[n, 2 * t + 1] = jnp.where(low, other, tile).astype(BF16)
 
 
-def row_attend(n, sp, x_ref, bias_ref, wo, qd, kk, vt, gt, mask, mid, mix):
+def row_attend(sp, dx, x_ref, bias_ref, wo, qd, kk, vt, gt, mask, mid, mix):
     low = lax.broadcasted_iota(jnp.int32, (D, 128), 1) < 64
-    halves = []
-    for e in range(2):
-        tile = qd[n, sp * 2 + e]
-        wide = jnp.concatenate([tile] * 4, axis=1) * mask[...]
-        bias = jnp.concatenate([bias_ref[t, sp, 2 * e : 2 * e + 2].reshape(512, 128) for t in range(4)], axis=1)
-        score = dot(kk[n], wide) + bias.astype(F32)
+    bias = jnp.concatenate(
+        [bias_ref[t, dx, 2 * e : 2 * e + 2].reshape(512, 128) for e in range(2) for t in range(4)], axis=1
+    ).astype(F32)
+    for n in range(2):
+        wide = jnp.concatenate([jnp.concatenate([qd[n, sp * 2 + e]] * 4, axis=1) * mask[...] for e in range(2)], axis=1)
+        score = dot(kk[n], wide) + bias
         peak = jnp.max(score, axis=0, keepdims=True)
         terms = jnp.exp(score - peak)
         scale = 1.0 / jnp.sum(terms, axis=0, keepdims=True)
         terms = terms.astype(BF16)
-        parts = []
-        for half in range(2):
-            o = dot(vt[n, half * 128 : half * 128 + 128, :], terms[:, half * 256 : half * 256 + 256])
-            o = o * scale[:, half * 256 : half * 256 + 256]
-            for h in range(4):
-                part = o[h * D : h * D + D, (h // 2) * 128 : (h // 2) * 128 + 128]
-                if h % 2 != e:
-                    part = pltpu.roll(part, 64, axis=1)
-                parts.append(part)
-        halves.append(parts)
-    ot = jnp.concatenate([jnp.where(low, a, b) for a, b in zip(*halves)], axis=0)
-    gated = (gt[n, sp].astype(F32) * ot).astype(BF16)
-    x = x_ref[pl.ds(sp * 4, 4), n].reshape(128, C).astype(F32)
-    new = x + dot_tn(gated, wo[...])
-    for ch in range(2):
-        mid[ch] = new[:, ch * 128 : ch * 128 + 128]
-    for ch in range(2):
-        for a in range(4):
-            mix[pl.ds(sp * 512 + n * 8 + ch * 4 + a, 32, stride=16), :] = mid[ch, pl.ds(a, 32, stride=4), :]
-
-
-def column_step(a, mix, wt, wk, wo, win, wout, wf, ot):
+        halves = []
+        for e in range(2):
+            parts = []
+            for half in range(2):
+                at = e * 512 + half * 256
+                o = dot(vt[n, half * 128 : half * 128 + 128, :], terms[:, at : at + 256]) * scale[:, at : at + 256]
+                for h in range(4):
+                    part = o[h * D : h * D + D, (h // 2) * 128 : (h // 2) * 128 + 128]
+                    if h % 2 != e:
+                        part = pltpu.roll(part, 64, axis=1)
+                    parts.append(part)
+            halves.append(parts)
+        ot = jnp.concatenate([jnp.where(low, a, b) for a, b in zip(*halves)], axis=0)
+        gated = (gt[n, sp].astype(F32) * ot).astype(BF16)
+        x = x_ref[pl.ds(sp * 4, 4), n].reshape(128, C).astype(F32)
+        new = x + dot_tn(gated, wo[...])
+        for ch in range(2):
+            mid[n, ch] = new[:, ch * 128 : ch * 128 + 128]
+        for ch in range(2):
+            for a in range(4):
+                mix[pl.ds(sp * 512 + n * 8 + ch * 4 + a, 32, stride=16), :] = mid[n, ch, pl.ds(a, 32, stride=4), :]
+
+
+def column_step(a, mix, wt, wk, wo, win, wout, wf):
     head = lax.broadcasted_iota(jnp.int32, (C, C), 0) // D
     cells = jnp.concatenate(
         [
@@ -133,14 +135,16 @@
         axis=0,
     )
     q, k, v, g = project(layer_norm(cells).astype(BF16), wt[...], wk)
-    for h in range(H):
-        one = jnp.where(head == h, q, jnp.zeros_like(q))
-        score = dot(k, one)
-        peak = jnp.max(score, axis=0, keepdims=True)
-        terms = jnp.exp(score - peak)
-        scale = 1.0 / jnp.sum(terms, axis=0, keepdims=True)
-        ot[h * D : h * D + D, :] = dot(v[h * D : h * D + D], terms.astype(BF16)) * scale
-    gated = (g.astype(F32) * ot[...]).astype(BF16)
+    wide = jnp.concatenate([jnp.where(head == h, q, jnp.zeros_like(q)) for h in range(H)], axis=1)
+    score = dot(k, wide)
+    peak = jnp.max(score, axis=0, keepdims=True)
+    terms = jnp.exp(score - peak)
+    scale = 1.0 / jnp.sum(terms, axis=0, keepdims=True)
+    terms = terms.astype(BF16)
+    ot = jnp.concatenate(
+        [dot(v[h * D : h * D + D], terms[:, h * C : h * C + C]) * scale[:, h * C : h * C + C] for h in range(H)], axis=0
+    )
+    gated = (g.astype(F32) * ot).astype(BF16)
     stream = cells + dot_tn(gated, wo[...])
     normed = layer_norm(stream).astype(BF16)
     hidden = jnp.maximum(dot(normed, win[...]), 0.0).astype(BF16)
@@ -190,9 +194,9 @@
     x_hbm, pair_hbm, bw_hbm, rw_hbm, ro_hbm, cw_hbm, co_hbm, ti_hbm, to_hbm, oi_hbm, oo_hbm,
     ao_hbm, pu_hbm,
     pair, bw, rw, ro, cw, co, ti, to, oi, oo,
-    own, xo, bias, qd, kk, vt, gt, mask, mid, mix, wt, sendbuf, cells, ot, fl, fr, lo, ri, left, wide, block, pairs,
+    own, xo, bias, qd, kk, vt, gt, mask, mid, mix, wt, sendbuf, cells, fl, fr, lo, ri, left, wide, block, pairs,
     ao, pu,
-    zsend, zrecv, ysend, yrecv, hrecv, srecv, lrecv, lsem,
+    zsend, zrecv, ysend, yrecv, tsend, trecv, hrecv, srecv, lrecv, lsem,
     hsend, ssend, xsend, xrecv, csend, crecv, lsend, fsend, frecv, rsend, rrecv,
 ):
     s, r = lax.axis_index("seq"), lax.axis_index("res")
@@ -223,62 +227,87 @@
     barrier = pltpu.get_barrier_semaphore()
 
     def greet(k, carry):
-        other = (here + k) % 128
-        pl.semaphore_signal(barrier, inc=1, device_id=(other // RES, other % RES), device_id_type=MESH)
+        pl.semaphore_signal(barrier, inc=1, device_id=(s, (r + k) % 16), device_id_type=MESH)
         return carry
 
-    lax.fori_loop(1, 128, greet, 0)
+    lax.fori_loop(1, 16, greet, 0)
+    for dim in "xy":
+        for by in (1, 2, 3):
+            pl.semaphore_signal(barrier, inc=1, device_id=near(dim, by), device_id_type=MESH)
 
     need("pair")
     need("bw")
     pair_bias(pair, bw, own)
-    mine_at = bias.at[:, pos["x"], pos["y"], pos["z"], core]
+    mine_at = bias.at[:, 0, pos["y"], pos["z"], core]
     place = pltpu.make_async_copy(own, mine_at, lsem.at[0])
     place.start()
-    pl.semaphore_wait(barrier, 127)
-
-    def scatter_x(k, carry):
-        other = (r + k) % 16
-        remote(x_hbm.at[other], xo.at[r], xsend, xrecv, (s, other)).start()
-        return carry
-
-    def line(x, y, ts=pl.ds(0, 4)):
-        return bias.at[ts, x, y, :, core]
-
-    def share(plane, what):
-        remote(what, what, ssend, srecv.at[plane], sibling).start()
-
-    parts = (pl.ds(0, 2), pl.ds(2, 2))
+    pl.semaphore_wait(barrier, 21)
+
+    def scatter_x(y_lo, first):
+        def one(k, carry):
+            other = y_lo * 8 + (r + k) % 8
+            remote(x_hbm.at[other], xo.at[r], xsend, xrecv, (s, other)).start()
+            return carry
+
+        lax.fori_loop(first, 8, one, 0)
+
     px, py, pz = pos["x"], pos["y"], pos["z"]
+    ALL, MOST = pl.ds(0, 4), pl.ds(0, 3)
+    REST = pl.ds(1, 3)
+    HALVES = (pl.ds(0, 2), pl.ds(2, 2))
+
+    def line(dx, y, ts=MOST, zs=ALL):
+        return bias.at[ts, dx, y, zs, core]
+
+    def share(group, what):
+        remote(what, what, ssend, srecv.at[group], sibling).start()
 
     def along_x(k, y):
         for way, by in enumerate((1, 3)):
-            remote(line(px, y), line(px, y), hsend, hrecv.at[k, way], near("x", by)).start()
+            remote(line(0, y), line(4 - by, y), hsend, hrecv.at[k, way], near("x", by)).start()
 
     def onward_x(k, y):
         for way, by in enumerate((1, 3)):
-            x = (px + (3, 1)[way]) % 4
-            remote(line(x, y), line(x, y), hsend, hrecv.at[k, way], near("x", by)).wait_recv()
-            part = line(x, y, parts[way])
-            remote(part, part, hsend, hrecv.at[k, 2 + way], near("x", by)).start()
-            share(1 + way, line(x, y))
+            got = line(4 - by, y)
+            remote(got, got, hsend, hrecv.at[k, way], near("x", by)).wait_recv()
+            remote(
+                line(4 - by, y, zs=HALVES[way]), line(2, y, zs=HALVES[way]), hsend, hrecv.at[k, 2 + way], near("x", by)
+            ).start()
+            share(4 - by, got)
 
     def last_x(k, y):
         for way, by in enumerate((1, 3)):
-            part = line((px + 2) % 4, y, parts[way])
+            part = line(2, y, zs=HALVES[way])
             remote(part, part, hsend, hrecv.at[k, 2 + way], near("x", by)).wait_recv()
-        share(3, line((px + 2) % 4, y))
-
-    def shared(plane, x):
-        half = bias.at[:, x, :, :, 1 - core]
-        remote(half, half, hsend, srecv.at[plane], sibling).wait_recv()
-
-    first_z = [
-        remote(own, bias.at[:, px, py, pz, core], zsend.at[k], zrecv.at[k], near("z", by)) for k, by in enumerate((1, 3, 2))
-    ]
-    for copy in first_z:
-        copy.start()
-    lax.fori_loop(1, 16, scatter_x, 0)
+        share(2, line(2, y))
+
+    def shared(group):
+        half = bias.at[ALL, 0, :, :, 1 - core] if group == 0 else bias.at[MOST, group, :, :, 1 - core]
+        if group == 4:
+            half = bias.at[3, REST, :, :, 1 - core]
+        remote(half, half, hsend, srecv.at[group], sibling).wait_recv()
+
+    def start(copies):
+        for copy in copies:
+            copy.start()
+        return copies
+
+    def arrived(copies):
+        for copy in copies:
+            copy.wait_recv()
+
+    BY = (1, 3, 2)
+    first_z = start(
+        [remote(own, bias.at[:, 0, py, pz, core], zsend.at[k], zrecv.at[k], near("z", by)) for k, by in enumerate(BY)]
+    )
+    t_x = start(
+        [
+            remote(own.at[3], bias.at[3, 4 - by, py, pz, core], tsend.at[k], trecv.at[k], near("x", by))
+            for k, by in enumerate(BY)
+        ]
+    )
+    y_lo = r // 8
+    scatter_x(y_lo, 1)
 
     row = lax.broadcasted_iota(jnp.int32, (C, 512), 0) // D
     lane = lax.broadcasted_iota(jnp.int32, (C, 512), 1) // 64
@@ -288,105 +317,107 @@
         wt[0, i * C : i * C + C, :] = rw[:, at * C : at * C + C].T
 
     place.wait()
-    for copy in first_z:
-        copy.wait_recv()
-    first_y = [
-        remote(line(px, py), line(px, py), ysend.at[k], yrecv.at[k], near("y", by)) for k, by in enumerate((1, 3))
-    ]
-    for copy in first_y:
-        copy.start()
+    arrived(first_z)
+    whole = line(0, py, ALL)
+    first_y = start([remote(whole, whole, ysend.at[k], yrecv.at[k], near("y", by)) for k, by in enumerate((1, 3))])
     along_x(0, py)
-    share(0, line(px, py))
+    share(0, whole)
+    scatter_x(1 - y_lo, 0)
+    arrived(t_x)
+    spot = bias.at[3, REST, py, pz, core]
+    t_y = start([remote(spot, spot, tsend.at[3 + k], trecv.at[3 + k], near("y", by)) for k, by in enumerate(BY)])
     need("cw")
     for i, at in enumerate((0, 2, 3)):
         wt[1, i * C : i * C + C, :] = cw[:, at * C : at * C + C].T
     second_y = []
     for k, by in enumerate((1, 3)):
         first_y[k].wait_recv()
-        y = (py + (3, 1)[k]) % 4
-        part = line(px, y, parts[k])
-        second_y.append(remote(part, part, ysend.at[2 + k], yrecv.at[2 + k], near("y", by)))
-        second_y[k].start()
+        y = (py + 4 - by) % 4
+        part = line(0, y, HALVES[k])
+        second_y += start([remote(part, part, ysend.at[2 + k], yrecv.at[2 + k], near("y", by))])
         along_x(1 + k, y)
-        share(0, line(px, y))
+        share(0, line(0, y, ALL))
     need("oo")
     outer_weight(oo, block)
-    for copy in second_y:
-        copy.wait_recv()
+    arrived(t_y)
+
+    def wall(z, ys=ALL):
+        return bias.at[3, REST, ys, z, core]
+
+    t_z = start(
+        [remote(wall(pz), wall(pz), tsend.at[6 + k], trecv.at[6 + k], near("z", by)) for k, by in enumerate((1, 3))]
+    )
+    share(4, wall(pz))
+    onward_x(0, py)
+    arrived(second_y)
     along_x(3, (py + 2) % 4)
-    share(0, line(px, (py + 2) % 4))
+    share(0, line(0, (py + 2) % 4, ALL))
     need("keep")
     most = xo.at[pl.ds(0, 15)]
     remote(most, most, xsend, xrecv, sibling).wait()
     row_project(0, xo, wt.at[0], rw[:, C : 2 * C], qd, kk, vt, gt)
-    onward_x(0, py)
+    onward_x(1, (py + 3) % 4)
+    onward_x(2, (py + 1) % 4)
+    for k, by in enumerate((1, 3)):
+        t_z[k].wait_recv()
+        z = (pz + 4 - by) % 4
+        part = wall(z, HALVES[k])
+        t_z += start([remote(part, part, tsend.at[8 + k], trecv.at[8 + k], near("z", by))])
+        share(4, wall(z))
     row_project(1, xo, wt.at[0], rw[:, C : 2 * C], qd, kk, vt, gt)
-    onward_x(1, (py + 3) % 4)
+    arrived(t_z[2:])
+    share(4, wall((pz + 2) % 4))
     need("ro")
 
-    def attend(index, carry):
-        q = index // 2
-        n = index % 2
-        sp = (px + q - q // 2 + 2 * (q % 2) * (1 - q // 2)) % 4
-
-        @pl.when(index == 0)
+    def attend(q, carry):
+        dx = q - q // 2 + 2 * (q % 2) * (1 - q // 2)
+        sp = (px + dx) % 4
+
+        @pl.when(q == 0)
         def _():
-            shared(0, px)
-
-        @pl.when(index == 1)
-        def _():
-            onward_x(2, (py + 1) % 4)
-
-        @pl.when(index == 2)
+            shared(0)
+
+        @pl.when(q == 1)
         def _():
             onward_x(3, (py + 2) % 4)
-            shared(1, (px + 3) % 4)
-
-        @pl.when(index == 3)
+            shared(4)
+            shared(3)
+
+        @pl.when(q == 2)
         def _():
             last_x(0, py)
-
-        @pl.when(index == 4)
-        def _():
-            shared(2, (px + 1) % 4)
-
-        @pl.when(index == 5)
-        def _():
             last_x(1, (py + 3) % 4)
-
-        @pl.when(index == 6)
+            shared(1)
+
+        @pl.when(q == 3)
         def _():
             last_x(2, (py + 1) % 4)
             last_x(3, (py + 2) % 4)
-            shared(3, (px + 2) % 4)
-
-        row_attend(n, sp, xo, bias, ro, qd, kk, vt, gt, mask, mid, mix)
-
-        @pl.when(n == 1)
-        def _():
-            rows = mix[pl.ds(pl.multiple_of(sp * 512, 512), 512), :].astype(BF16)
-            sendbuf[pl.ds(sp * 32, 32)] = rows.reshape(32, 16, 128)
-
-            def scatter(i, carry):
-                other = sp * 32 + (here + i) % 32
-
-                @pl.when(other != here)
-                def _():
-                    remote(sendbuf.at[other], cells.at[here], csend, crecv, (other // RES, other % RES)).start()
-
-                return carry
-
-            lax.fori_loop(0, 32, scatter, 0)
-
+            shared(2)
+
+        row_attend(sp, dx, xo, bias, ro, qd, kk, vt, gt, mask, mid, mix)
+        rows = mix[pl.ds(pl.multiple_of(sp * 512, 512), 512), :].astype(BF16)
+        sendbuf[pl.ds(sp * 32, 32)] = rows.reshape(32, 16, 128)
+
+        def scatter(i, carry):
+            other = sp * 32 + (here + i) % 32
+
+            @pl.when(other != here)
+            def _():
+                remote(sendbuf.at[other], cells.at[here], csend, crecv, (other // RES, other % RES)).start()
+
+            return carry
+
+        lax.fori_loop(0, 32, scatter, 0)
         return carry
 
-    lax.fori_loop(0, 8, attend, 0)
+    lax.fori_loop(0, 4, attend, 0)
     cells[here] = sendbuf[here]
-    for copy in first_z + first_y + second_y:
+    for copy in first_z + first_y + second_y + t_x + t_y + t_z:
         copy.wait_send()
     most = bias.at[:, :, :, :, 0]
     remote(most, most, ssend, srecv.at[0], sibling).wait_send()
-    most = bias.at[:, pl.ds(0, 3), :, :, 0]
+    most = bias.at[MOST, MOST, :, :, 0]
     remote(most, most, hsend, srecv.at[0], sibling).wait_send()
     for name in ("co", "ti", "to", "oi"):
         need(name)
@@ -406,7 +437,7 @@
         remote(line, line, fsend, frecv, sibling).start()
 
     def residue(a, carry):
-        factor = column_step(a, mix, wt.at[1], cw[:, C : 2 * C], co, ti, to, wf, ot)
+        factor = column_step(a, mix, wt.at[1], cw[:, C : 2 * C], co, ti, to, wf)
         fl[a] = factor[:D]
         fr[a] = factor[D:]
         lo[chip, core, a] = factor[:D]
@@ -436,7 +467,9 @@
         return carry
 
     lax.fori_loop(0, 4, residue, 0)
-    ao[...] = mix[...].astype(BF16)
+    new = mix[...].astype(BF16).reshape(256, 8, 128)
+    for ch in range(2):
+        ao[:, :, ch * 128 : ch * 128 + 128] = new[:, ch * 4 : ch * 4 + 4, :]
     save = pltpu.make_async_copy(ao, ao_hbm, lsem.at[0])
     save.start()
     onward_left(3)
@@ -477,7 +510,7 @@
     dma = pltpu.SemaphoreType.DMA
     new, update = pl.pallas_call(
         whole_kernel,
-        out_shape=(jax.ShapeDtypeStruct((2048, 128), BF16), jax.ShapeDtypeStruct((2048, 128), BF16)),
+        out_shape=(jax.ShapeDtypeStruct((256, 4, C), BF16), jax.ShapeDtypeStruct((2048, 128), BF16)),
         in_specs=[ANY] * 11,
         out_specs=(ANY, ANY),
         scratch_shapes=[
@@ -499,12 +532,11 @@
             pltpu.VMEM((2, C, 512), BF16),
             pltpu.VMEM((2, 4, C, 128), BF16),
             pltpu.VMEM((C, 512), BF16),
-            pltpu.VMEM((2, 128, 128), F32),
+            pltpu.VMEM((2, 2, 128, 128), F32),
             pltpu.VMEM((2048, 128), F32),
             pltpu.VMEM((2, 3 * C, C), BF16),
             pltpu.VMEM((128, 16, 128), BF16),
             pltpu.VMEM((128, 16, 128), BF16),
-            pltpu.VMEM((C, 256), F32),
             pltpu.VMEM((4, D, 256), BF16),
             pltpu.VMEM((4, D, 256), BF16),
             pltpu.VMEM((8, 2, 4, D, 256), BF16),
@@ -513,14 +545,16 @@
             pltpu.VMEM((512, 4096), BF16),
             pltpu.VMEM((4096, 512), BF16),
             pltpu.VMEM((2048, 128), F32),
-            pltpu.VMEM((2048, 128), BF16),
+            pltpu.VMEM((256, 4, C), BF16),
             pltpu.VMEM((2048, 128), BF16),
             dma((3,)),
             dma((3,)),
             dma((4,)),
             dma((4,)),
+            dma((10,)),
+            dma((10,)),
             dma((4, 4)),
-            dma((4,)),
+            dma((5,)),
             dma((4,)),
             dma((11,)),
         ]
@@ -541,8 +575,7 @@
         outer_out,
     )
     pair_update = update.reshape(64, 32, 128)
-    alignment_out = new.reshape(128, 2, 2, 4, 128).transpose(0, 1, 3, 2, 4).reshape(256, 4, C)
-    return (alignment_out, pair_update)
+    return (new, pair_update)
 
 
 def solution(mesh):

time: 89.9 us -> 85.3 us (0.949)
  Pallas kernels: 86.3 us -> 81.6 us
    pallas_call x1, Pallas kernels: 86.3 us -> 81.6 us  [body(): pl.pallas_call(whole_kernel, out_shape=(jax.ShapeDtypeStruct((256, 4, C),...]
where the time goes in v4:
time: 85.3 us; the launch traced here: 85.2 us
  Pallas kernels  81.6 us (96%)
  local copies, waits for them, and re-layouts  2.87 us (3%)
    pallas_call x1, Pallas kernels, body(): pl.pallas_call(whole_kernel, out_shape=(jax.ShapeDtypeStruct((256, 4, C),...  81.6 us
    unnamed x4, local copies, waits for them, and re-layouts  2.87 us

profile of v4, /device:TPU:1, one launch (start us, length us, event | category | flops | bytes accessed | tf_op | source)
XLA Modules:
  0.0 85.2 jit_solution(2576937633921050794)
XLA Ops:
  0.6 81.6 %evoformer.1 = (bf16[256,4,256]{2,1,0:T(4,128)(2,1)}, bf16[2048,128]{1,0:T(8,128)(2,1)}) custom-call(bf16[16,2,32,256]{3,2,1,0:T(8,128)(2,1)} %bitcast.4, bf16[64,32,128]{2,1,0:T(8,128)(2,1)} %pair_hbm.1, bf16[8,128]{1,0:T(8,128)(2,1)} %bitcast.7, bf16[256,1024]{1,0:T(8,128)(2,1)} %rw_hbm.1, bf16[256,256]{1,0:T(8,128)(2,1)} %ro_hbm.1, ...), custom_call_target="tpu_custom_call" | custom-call | tf_op jit(solution)/shard_map/evoformer/pallas_call | solution.py:511
  82.3 0.0 copy-start
  82.3 2.1 %copy.15 = bf16[256,4,256]{2,1,0:T(4,128)(2,1)} copy(bf16[256,4,256]{2,1,0:T(4,128)(2,1)} %get-tuple-element.8) | data formatting | bytes 1048576
  84.4 0.0 copy-done
  84.4 0.8 copy.16
Async XLA Ops:
  82.3 2.1 %copy-start = (bf16[2048,128]{1,0:T(8,128)(2,1)S(1)}, bf16[2048,128]{1,0:T(8,128)(2,1)}, u32[]{:S(2)}) copy-start(bf16[2048,128]{1,0:T(8,128)(2,1)} %get-tuple-element.5) | copy-start | bytes 1572868

commit v5 on v4

--- a/solution.py
+++ b/solution.py
@@ -196,7 +196,7 @@
     pair, bw, rw, ro, cw, co, ti, to, oi, oo,
     own, xo, bias, qd, kk, vt, gt, mask, mid, mix, wt, sendbuf, cells, fl, fr, lo, ri, left, wide, block, pairs,
     ao, pu,
-    zsend, zrecv, ysend, yrecv, tsend, trecv, hrecv, srecv, lrecv, lsem,
+    nsend, nrecv, hrecv, srecv, lrecv, lsem,
     hsend, ssend, xsend, xrecv, csend, crecv, lsend, fsend, frecv, rsend, rrecv,
 ):
     s, r = lax.axis_index("seq"), lax.axis_index("res")
@@ -243,43 +243,47 @@
     place.start()
     pl.semaphore_wait(barrier, 21)
 
-    def scatter_x(y_lo, first):
-        def one(k, carry):
-            other = y_lo * 8 + (r + k) % 8
-            remote(x_hbm.at[other], xo.at[r], xsend, xrecv, (s, other)).start()
-            return carry
-
-        lax.fori_loop(first, 8, one, 0)
+    def scatter_x(k, carry):
+        other = (r + k) % 16
+        remote(x_hbm.at[other], xo.at[r], xsend, xrecv, (s, other)).start()
+        return carry
 
     px, py, pz = pos["x"], pos["y"], pos["z"]
-    ALL, MOST = pl.ds(0, 4), pl.ds(0, 3)
-    REST = pl.ds(1, 3)
-    HALVES = (pl.ds(0, 2), pl.ds(2, 2))
-
-    def line(dx, y, ts=MOST, zs=ALL):
-        return bias.at[ts, dx, y, zs, core]
+    ALL, MOST, REST = pl.ds(0, 4), pl.ds(0, 3), pl.ds(1, 3)
+    LOW, HIGH = pl.ds(0, 2), pl.ds(2, 2)
+    HALVES = (LOW, HIGH)
+    BY = (1, 3, 2)
+    PARTS = [(kind, by) for by in (0, 3, 1, 2) for kind in "yz"]
+
+    def part_of(dx, k, inner=ALL):
+        kind, by = PARTS[k]
+        if kind == "y":
+            return bias.at[LOW, dx, (py + by) % 4, inner, core]
+        return bias.at[2, dx, inner, (pz + by) % 4, core]
 
     def share(group, what):
         remote(what, what, ssend, srecv.at[group], sibling).start()
 
-    def along_x(k, y):
+    def along_x(k):
         for way, by in enumerate((1, 3)):
-            remote(line(0, y), line(4 - by, y), hsend, hrecv.at[k, way], near("x", by)).start()
-
-    def onward_x(k, y):
-        for way, by in enumerate((1, 3)):
-            got = line(4 - by, y)
-            remote(got, got, hsend, hrecv.at[k, way], near("x", by)).wait_recv()
-            remote(
-                line(4 - by, y, zs=HALVES[way]), line(2, y, zs=HALVES[way]), hsend, hrecv.at[k, 2 + way], near("x", by)
-            ).start()
-            share(4 - by, got)
-
-    def last_x(k, y):
-        for way, by in enumerate((1, 3)):
-            part = line(2, y, zs=HALVES[way])
-            remote(part, part, hsend, hrecv.at[k, 2 + way], near("x", by)).wait_recv()
-        share(2, line(2, y))
+            remote(part_of(0, k), part_of(4 - by, k), hsend, hrecv.at[k, way], near("x", by)).start()
+
+    def onward_x(*ks):
+        for k in ks:
+            for way, by in enumerate((1, 3)):
+                got = part_of(4 - by, k)
+                remote(got, got, hsend, hrecv.at[k, way], near("x", by)).wait_recv()
+                remote(
+                    part_of(4 - by, k, HALVES[way]), part_of(2, k, HALVES[way]), hsend, hrecv.at[k, 2 + way], near("x", by)
+                ).start()
+                share(4 - by, got)
+
+    def last_x(*ks):
+        for k in ks:
+            for way, by in enumerate((1, 3)):
+                half = part_of(2, k, HALVES[way])
+                remote(half, half, hsend, hrecv.at[k, 2 + way], near("x", by)).wait_recv()
+            share(2, part_of(2, k))
 
     def shared(group):
         half = bias.at[ALL, 0, :, :, 1 - core] if group == 0 else bias.at[MOST, group, :, :, 1 - core]
@@ -287,86 +291,71 @@
             half = bias.at[3, REST, :, :, 1 - core]
         remote(half, half, hsend, srecv.at[group], sibling).wait_recv()
 
-    def start(copies):
-        for copy in copies:
+    copies = []
+
+    def three(dim, src, dst, base):
+        made = [remote(src, dst, nsend.at[base + k], nrecv.at[base + k], near(dim, by)) for k, by in enumerate(BY)]
+        for copy in made:
             copy.start()
-        return copies
-
-    def arrived(copies):
-        for copy in copies:
+        copies.extend(made)
+        return made
+
+    def arrived(made):
+        for copy in made:
             copy.wait_recv()
 
-    BY = (1, 3, 2)
-    first_z = start(
-        [remote(own, bias.at[:, 0, py, pz, core], zsend.at[k], zrecv.at[k], near("z", by)) for k, by in enumerate(BY)]
-    )
-    t_x = start(
-        [
-            remote(own.at[3], bias.at[3, 4 - by, py, pz, core], tsend.at[k], trecv.at[k], near("x", by))
-            for k, by in enumerate(BY)
-        ]
-    )
-    y_lo = r // 8
-    scatter_x(y_lo, 1)
-
+    low_z = three("z", own.at[LOW], bias.at[LOW, 0, py, pz, core], 0)
+    high_y = three("y", own.at[HIGH], bias.at[HIGH, 0, py, pz, core], 3)
+    t_x = []
+    for k, by in enumerate(BY):
+        t_x.append(remote(own.at[3], bias.at[3, 4 - by, py, pz, core], nsend.at[6 + k], nrecv.at[6 + k], near("x", by)))
+        t_x[k].start()
+    copies.extend(t_x)
+    lax.fori_loop(1, 16, scatter_x, 0)
+
+    place.wait()
+    arrived(low_z)
+    mine = bias.at[LOW, 0, py, :, core]
+    low_y = three("y", mine, mine, 9)
+    along_x(0)
+    arrived(high_y)
+    mine = bias.at[HIGH, 0, :, pz, core]
+    high_z = three("z", mine, mine, 12)
+    along_x(1)
+    arrived(t_x)
+    mine = bias.at[3, REST, py, pz, core]
+    t_y = three("y", mine, mine, 15)
     row = lax.broadcasted_iota(jnp.int32, (C, 512), 0) // D
     lane = lax.broadcasted_iota(jnp.int32, (C, 512), 1) // 64
     mask[...] = jnp.where(row == lane, 1.0, 0.0).astype(BF16)
     need("rw")
     for i, at in enumerate((0, 2, 3)):
         wt[0, i * C : i * C + C, :] = rw[:, at * C : at * C + C].T
-
-    place.wait()
-    arrived(first_z)
-    whole = line(0, py, ALL)
-    first_y = start([remote(whole, whole, ysend.at[k], yrecv.at[k], near("y", by)) for k, by in enumerate((1, 3))])
-    along_x(0, py)
-    share(0, whole)
-    scatter_x(1 - y_lo, 0)
-    arrived(t_x)
-    spot = bias.at[3, REST, py, pz, core]
-    t_y = start([remote(spot, spot, tsend.at[3 + k], trecv.at[3 + k], near("y", by)) for k, by in enumerate(BY)])
-    need("cw")
-    for i, at in enumerate((0, 2, 3)):
-        wt[1, i * C : i * C + C, :] = cw[:, at * C : at * C + C].T
-    second_y = []
-    for k, by in enumerate((1, 3)):
-        first_y[k].wait_recv()
-        y = (py + 4 - by) % 4
-        part = line(0, y, HALVES[k])
-        second_y += start([remote(part, part, ysend.at[2 + k], yrecv.at[2 + k], near("y", by))])
-        along_x(1 + k, y)
-        share(0, line(0, y, ALL))
-    need("oo")
-    outer_weight(oo, block)
+    for k in range(3):
+        low_y[k].wait_recv()
+        along_x(2 + 2 * k)
+        high_z[k].wait_recv()
+        along_x(3 + 2 * k)
+        if k == 0:
+            onward_x(0, 1)
+    share(0, bias.at[:, 0, :, :, core])
     arrived(t_y)
-
-    def wall(z, ys=ALL):
-        return bias.at[3, REST, ys, z, core]
-
-    t_z = start(
-        [remote(wall(pz), wall(pz), tsend.at[6 + k], trecv.at[6 + k], near("z", by)) for k, by in enumerate((1, 3))]
-    )
-    share(4, wall(pz))
-    onward_x(0, py)
-    arrived(second_y)
-    along_x(3, (py + 2) % 4)
-    share(0, line(0, (py + 2) % 4, ALL))
+    mine = bias.at[3, REST, :, pz, core]
+    t_z = three("z", mine, mine, 18)
     need("keep")
     most = xo.at[pl.ds(0, 15)]
     remote(most, most, xsend, xrecv, sibling).wait()
     row_project(0, xo, wt.at[0], rw[:, C : 2 * C], qd, kk, vt, gt)
-    onward_x(1, (py + 3) % 4)
-    onward_x(2, (py + 1) % 4)
-    for k, by in enumerate((1, 3)):
-        t_z[k].wait_recv()
-        z = (pz + 4 - by) % 4
-        part = wall(z, HALVES[k])
-        t_z += start([remote(part, part, tsend.at[8 + k], trecv.at[8 + k], near("z", by))])
-        share(4, wall(z))
+    onward_x(2, 3)
     row_project(1, xo, wt.at[0], rw[:, C : 2 * C], qd, kk, vt, gt)
-    arrived(t_z[2:])
-    share(4, wall((pz + 2) % 4))
+    onward_x(4, 5)
+    need("oo")
+    outer_weight(oo, block)
+    need("cw")
+    for i, at in enumerate((0, 2, 3)):
+        wt[1, i * C : i * C + C, :] = cw[:, at * C : at * C + C].T
+    arrived(t_z)
+    share(4, bias.at[3, REST, :, :, core])
     need("ro")
 
     def attend(q, carry):
@@ -379,41 +368,44 @@
 
         @pl.when(q == 1)
         def _():
-            onward_x(3, (py + 2) % 4)
+            onward_x(6, 7)
+            last_x(0, 1)
             shared(4)
             shared(3)
 
         @pl.when(q == 2)
         def _():
-            last_x(0, py)
-            last_x(1, (py + 3) % 4)
+            last_x(2, 3, 4, 5)
             shared(1)
 
         @pl.when(q == 3)
         def _():
-            last_x(2, (py + 1) % 4)
-            last_x(3, (py + 2) % 4)
+            last_x(6, 7)
             shared(2)
 
         row_attend(sp, dx, xo, bias, ro, qd, kk, vt, gt, mask, mid, mix)
         rows = mix[pl.ds(pl.multiple_of(sp * 512, 512), 512), :].astype(BF16)
         sendbuf[pl.ds(sp * 32, 32)] = rows.reshape(32, 16, 128)
 
-        def scatter(i, carry):
-            other = sp * 32 + (here + i) % 32
-
-            @pl.when(other != here)
-            def _():
-                remote(sendbuf.at[other], cells.at[here], csend, crecv, (other // RES, other % RES)).start()
-
-            return carry
-
-        lax.fori_loop(0, 32, scatter, 0)
+        for yh in range(2):
+            to_s = sp * 2 + yh
+
+            def scatter(i, carry):
+                to_r = lax.bitwise_and(r + i, 15)
+                other = to_s * 16 + to_r
+
+                @pl.when(other != here)
+                def _():
+                    remote(sendbuf.at[other], cells.at[here], csend, crecv, (to_s, to_r)).start()
+
+                return carry
+
+            lax.fori_loop(0, 16, scatter, 0, unroll=True)
         return carry
 
     lax.fori_loop(0, 4, attend, 0)
     cells[here] = sendbuf[here]
-    for copy in first_z + first_y + second_y + t_x + t_y + t_z:
+    for copy in copies:
         copy.wait_send()
     most = bias.at[:, :, :, :, 0]
     remote(most, most, ssend, srecv.at[0], sibling).wait_send()
@@ -447,18 +439,18 @@
             ri[r % 8, a] = factor[D:]
 
         def send_left(k, carry):
-            remote(fl.at[a], lo.at[chip, core, a], lsend, lrecv.at[a], (s, ((chip + k) % 8) * 2 + core)).start()
+            remote(fl.at[a], lo.at[chip, core, a], lsend, lrecv.at[a], (s, lax.bitwise_and(chip + k, 7) * 2 + core)).start()
             return carry
 
         def send_right(k, carry):
             @pl.when(jnp.logical_not(jnp.logical_and(is_own, k == 0)))
             def _():
-                remote(fr.at[a], ri.at[r % 8, a], rsend, rrecv, ((s + k) % 8, column)).start()
+                remote(fr.at[a], ri.at[r % 8, a], rsend, rrecv, (lax.bitwise_and(s + k, 7), column)).start()
 
             return carry
 
-        lax.fori_loop(1, 8, send_left, 0)
-        lax.fori_loop(0, 8, send_right, 0)
+        lax.fori_loop(1, 8, send_left, 0, unroll=True)
+        lax.fori_loop(0, 8, send_right, 0, unroll=True)
 
         @pl.when(a > 0)
         def _():
@@ -547,13 +539,9 @@
             pltpu.VMEM((2048, 128), F32),
             pltpu.VMEM((256, 4, C), BF16),
             pltpu.VMEM((2048, 128), BF16),
-            dma((3,)),
-            dma((3,)),
-            dma((4,)),
-            dma((4,)),
-            dma((10,)),
-            dma((10,)),
-            dma((4, 4)),
+            dma((21,)),
+            dma((21,)),
+            dma((8, 4)),
             dma((5,)),
             dma((4,)),
             dma((11,)),

time: 85.3 us -> 79.2 us (0.928)
  Pallas kernels: 81.6 us -> 75.5 us
    pallas_call x1, Pallas kernels: 81.6 us -> 75.5 us  [body(): pl.pallas_call(whole_kernel, out_shape=(jax.ShapeDtypeStruct((256, 4, C),...]
where the time goes in v5:
time: 79.2 us; the launch traced here: 79 us
  Pallas kernels  75.5 us (95%)
  local copies, waits for them, and re-layouts  2.87 us (4%)
    pallas_call x1, Pallas kernels, body(): pl.pallas_call(whole_kernel, out_shape=(jax.ShapeDtypeStruct((256, 4, C),...  75.5 us
    unnamed x4, local copies, waits for them, and re-layouts  2.87 us

profile of v5, /device:TPU:1, one launch (start us, length us, event | category | flops | bytes accessed | tf_op | source)
XLA Modules:
  0.0 79.0 jit_solution(963628398650191600)
XLA Ops:
  0.6 75.5 %evoformer.1 = (bf16[256,4,256]{2,1,0:T(4,128)(2,1)}, bf16[2048,128]{1,0:T(8,128)(2,1)}) custom-call(bf16[16,2,32,256]{3,2,1,0:T(8,128)(2,1)} %bitcast.4, bf16[64,32,128]{2,1,0:T(8,128)(2,1)} %pair_hbm.1, bf16[8,128]{1,0:T(8,128)(2,1)} %bitcast.7, bf16[256,1024]{1,0:T(8,128)(2,1)} %rw_hbm.1, bf16[256,256]{1,0:T(8,128)(2,1)} %ro_hbm.1, ...), custom_call_target="tpu_custom_call" | custom-call | tf_op jit(solution)/shard_map/evoformer/pallas_call | solution.py:503
  76.1 0.0 copy-start
  76.2 2.1 %copy.15 = bf16[256,4,256]{2,1,0:T(4,128)(2,1)} copy(bf16[256,4,256]{2,1,0:T(4,128)(2,1)} %get-tuple-element.8) | data formatting | bytes 1048576
  78.2 0.0 copy-done
  78.2 0.8 %copy.16 = bf16[64,32,128]{2,1,0:T(8,128)(2,1)} copy(bf16[64,32,128]{2,1,0:T(8,128)(2,1)S(1)} %bitcast.5) | data formatting | bytes 1048576
Async XLA Ops:
  76.1 2.1 %copy-start = (bf16[2048,128]{1,0:T(8,128)(2,1)S(1)}, bf16[2048,128]{1,0:T(8,128)(2,1)}, u32[]{:S(2)}) copy-start(bf16[2048,128]{1,0:T(8,128)(2,1)} %get-tuple-element.5) | copy-start | bytes 1572868

commit v6 on v5

--- a/solution.py
+++ b/solution.py
@@ -165,39 +165,61 @@
             block[c * 128 + j * 32 : c * 128 + j * 32 + 32, j * 128 : j * 128 + 128] = one
 
 
-def outer_part(left_ref, right_ref, out_ref, left, wide, block, pairs):
+def outer_left(a, left_ref, left):
     for n in range(2):
-        left[n] = left_ref[:, :, :, :, n * 128 : n * 128 + 128].reshape(2048, 128).astype(F32)
-    right = right_ref[...].reshape(1024, 256)
-    for c in range(0, 32, 2):
+        left[n, a] = left_ref[:, :, a, :, n * 128 : n * 128 + 128].reshape(512, 128).astype(F32)
+
+
+def outer_right(a, right_ref, right):
+    right[a] = right_ref[:, a].reshape(256, 256).T
+
+
+def outer_products(las, ras, left, right, wide):
+    count = 16 * len(las)
+    for first in range(0, 32, 8):
         rows = jnp.concatenate(
             [
-                jnp.concatenate([left[n, pl.ds(c + k, 64, stride=32), :] for n in range(2)], axis=1)
-                for k in range(2)
+                jnp.concatenate([left[n, a, pl.ds(c, 16, stride=32), :] for n in range(2)], axis=1)
+                for c in range(first, first + 8)
+                for a in las
             ],
             axis=0,
-        )
-        product = (dot_nt(rows.astype(BF16), right) * (1.0 / 256)).astype(BF16)
-        for k in range(2):
-            for g in range(8):
-                wide[g * 64 : g * 64 + 64, (c + k) * 128 : (c + k) * 128 + 128] = product[
-                    k * 64 : k * 64 + 64, g * 128 : g * 128 + 128
-                ]
-    update = dot(wide[...], block[...])
-    for g in range(8):
-        for j in range(4):
-            pairs[pl.ds(g * 4 + j, 64, stride=32), :] = update[g * 64 : g * 64 + 64, j * 128 : j * 128 + 128]
-    out_ref[...] = pairs[...].astype(BF16)
+        ).astype(BF16)
+        for ra in ras:
+            product = (dot(rows, right[ra]) * (1.0 / 256)).astype(BF16)
+            for c in range(8):
+                for half in range(2):
+                    at = (first + c) * 128
+                    wide[ra * 2 + half, las[0] * 16 : las[0] * 16 + count, at : at + 128] = product[
+                        c * count : c * count + count, half * 128 : half * 128 + 128
+                    ]
+
+
+def outer_update(groups, las, wide, block, pairs):
+    parts = []
+    for (low, high), some in zip(groups, las):
+        count = 16 * len(some)
+        parts.append(wide[low:high, some[0] * 16 : some[0] * 16 + count, :].reshape((high - low) * count, 4096))
+    update = dot(jnp.concatenate(parts, axis=0), block[...])
+    at = 0
+    for (low, high), some in zip(groups, las):
+        for g in range(low, high):
+            for a in some:
+                for o in range(4):
+                    pairs[pl.ds(a * 32 + (g % 2) * 16 + o * 4 + g // 2, 16, stride=128), :] = update[
+                        at : at + 16, o * 128 : o * 128 + 128
+                    ]
+                at += 16
 
 
 def whole_kernel(
     x_hbm, pair_hbm, bw_hbm, rw_hbm, ro_hbm, cw_hbm, co_hbm, ti_hbm, to_hbm, oi_hbm, oo_hbm,
     ao_hbm, pu_hbm,
     pair, bw, rw, ro, cw, co, ti, to, oi, oo,
-    own, xo, bias, qd, kk, vt, gt, mask, mid, mix, wt, sendbuf, cells, fl, fr, lo, ri, left, wide, block, pairs,
+    own, xo, bias, qd, kk, vt, gt, mask, mid, mix, wt, sendbuf, cells, fl, fr, lo, ri, left, right, wide, block, pairs,
     ao, pu,
-    nsend, nrecv, hrecv, srecv, lrecv, lsem,
-    hsend, ssend, xsend, xrecv, csend, crecv, lsend, fsend, frecv, rsend, rrecv,
+    nsend, nrecv, hrecv, srecv, lrecv, frecv, rrecv, lsem,
+    hsend, ssend, xsend, xrecv, csend, crecv, lsend, fsend, rsend,
 ):
     s, r = lax.axis_index("seq"), lax.axis_index("res")
     here = s * RES + r
@@ -426,7 +448,7 @@
         most = lo.at[pl.ds(0, 7), core, a]
         remote(most, most, lsend, lrecv.at[a], sibling).wait_recv()
         line = lo.at[:, core, a]
-        remote(line, line, fsend, frecv, sibling).start()
+        remote(line, line, fsend, frecv.at[a], sibling).start()
 
     def residue(a, carry):
         factor = column_step(a, mix, wt.at[1], cw[:, C : 2 * C], co, ti, to, wf)
@@ -445,7 +467,7 @@
         def send_right(k, carry):
             @pl.when(jnp.logical_not(jnp.logical_and(is_own, k == 0)))
             def _():
-                remote(fr.at[a], ri.at[r % 8, a], rsend, rrecv, (lax.bitwise_and(s + k, 7), column)).start()
+                remote(fr.at[a], ri.at[r % 8, a], rsend, rrecv.at[a], (lax.bitwise_and(s + k, 7), column)).start()
 
             return carry
 
@@ -464,22 +486,48 @@
         ao[:, :, ch * 128 : ch * 128 + 128] = new[:, ch * 4 : ch * 4 + 4, :]
     save = pltpu.make_async_copy(ao, ao_hbm, lsem.at[0])
     save.start()
+
+    def gathered(a):
+        half = lo.at[:, 1 - core, a]
+        remote(half, half, fsend, frecv.at[a], sibling).wait_recv()
+
+        @pl.when(is_own)
+        def _():
+            part = ri.at[pl.ds(0, 7), a]
+            remote(part, part, rsend, rrecv.at[a], sibling).wait_recv()
+
+        @pl.when(jnp.logical_not(is_own))
+        def _():
+            part = ri.at[:, a]
+            remote(part, part, rsend, rrecv.at[a], sibling).wait_recv()
+
+        outer_left(a, lo, left)
+        outer_right(a, ri, right)
+
+    for a in range(3):
+        gathered(a)
+    outer_products((0, 1, 2), (0, 1, 2), left, right, wide)
     onward_left(3)
+    outer_update(((0, 6),), ((0, 1, 2),), wide, block, pairs)
+    gathered(3)
+    outer_products((3,), (0, 1, 2, 3), left, right, wide)
+    outer_products((0, 1, 2), (3,), left, right, wide)
+    outer_update(((0, 8), (6, 8)), ((3,), (0, 1, 2)), wide, block, pairs)
+    pu[...] = pairs[...].astype(BF16)
     most = lo.at[pl.ds(0, 7), core]
-    remote(most, most, lsend, frecv, sibling).wait_send()
+    remote(most, most, lsend, lrecv.at[0], sibling).wait_send()
     half = lo.at[:, 1 - core]
-    remote(half, half, fsend, frecv, sibling).wait()
+    remote(half, half, fsend, lrecv.at[0], sibling).wait_send()
 
     @pl.when(is_own)
     def _():
         part = ri.at[pl.ds(0, 7)]
-        remote(part, part, rsend, rrecv, sibling).wait()
+        remote(part, part, rsend, lrecv.at[0], sibling).wait_send()
 
     @pl.when(jnp.logical_not(is_own))
     def _():
-        remote(ri, ri, rsend, rrecv, sibling).wait()
-
-    outer_part(lo, ri, pu, left, wide, block, pairs)
+        remote(ri, ri, rsend, lrecv.at[0], sibling).wait_send()
+
     last = pltpu.make_async_copy(pu, pu_hbm, lsem.at[1])
     last.start()
     last.wait()
@@ -533,8 +581,9 @@
             pltpu.VMEM((4, D, 256), BF16),
             pltpu.VMEM((8, 2, 4, D, 256), BF16),
             pltpu.VMEM((8, 4, D, 256), BF16),
-            pltpu.VMEM((2, 2048, 128), F32),
-            pltpu.VMEM((512, 4096), BF16),
+            pltpu.VMEM((2, 4, 512, 128), F32),
+            pltpu.VMEM((4, 256, 256), BF16),
+            pltpu.VMEM((8, 64, 4096), BF16),
             pltpu.VMEM((4096, 512), BF16),
             pltpu.VMEM((2048, 128), F32),
             pltpu.VMEM((256, 4, C), BF16),
@@ -544,9 +593,11 @@
             dma((8, 4)),
             dma((5,)),
             dma((4,)),
+            dma((4,)),
+            dma((4,)),
             dma((11,)),
         ]
-        + [dma] * 11,
+        + [dma] * 9,
         compiler_params=pltpu.CompilerParams(collective_id=0, has_side_effects=True, vmem_limit_bytes=56 << 20),
         name="evoformer",
     )(

time: 79.2 us -> 75.8 us (0.957)
  Pallas kernels: 75.5 us -> 72.1 us
    pallas_call x1, Pallas kernels: 75.5 us -> 72.1 us  [body(): pl.pallas_call(whole_kernel, out_shape=(jax.ShapeDtypeStruct((256, 4, C),...]
where the time goes in v6:
time: 75.8 us; the launch traced here: 75.6 us
  Pallas kernels  72.1 us (95%)
  local copies, waits for them, and re-layouts  2.87 us (4%)
    pallas_call x1, Pallas kernels, body(): pl.pallas_call(whole_kernel, out_shape=(jax.ShapeDtypeStruct((256, 4, C),...  72.1 us
    unnamed x4, local copies, waits for them, and re-layouts  2.87 us

profile of v6, /device:TPU:1, one launch (start us, length us, event | category | flops | bytes accessed | tf_op | source)
XLA Modules:
  0.0 75.6 jit_solution(29699655874817533)
XLA Ops:
  0.6 72.1 %evoformer.1 = (bf16[256,4,256]{2,1,0:T(4,128)(2,1)}, bf16[2048,128]{1,0:T(8,128)(2,1)}) custom-call(bf16[16,2,32,256]{3,2,1,0:T(8,128)(2,1)} %bitcast.4, bf16[64,32,128]{2,1,0:T(8,128)(2,1)} %pair_hbm.1, bf16[8,128]{1,0:T(8,128)(2,1)} %bitcast.7, bf16[256,1024]{1,0:T(8,128)(2,1)} %rw_hbm.1, bf16[256,256]{1,0:T(8,128)(2,1)} %ro_hbm.1, ...), custom_call_target="tpu_custom_call" | custom-call | tf_op jit(solution)/shard_map/evoformer/pallas_call | solution.py:551
  72.7 0.0 copy-start
  72.8 2.1 %copy.15 = bf16[256,4,256]{2,1,0:T(4,128)(2,1)} copy(bf16[256,4,256]{2,1,0:T(4,128)(2,1)} %get-tuple-element.8) | data formatting | bytes 1048576
  74.8 0.0 copy-done
  74.8 0.8 %copy.16 = bf16[64,32,128]{2,1,0:T(8,128)(2,1)} copy(bf16[64,32,128]{2,1,0:T(8,128)(2,1)S(1)} %bitcast.5) | data formatting | bytes 1048576
Async XLA Ops:
  72.7 2.1 %copy-start = (bf16[2048,128]{1,0:T(8,128)(2,1)S(1)}, bf16[2048,128]{1,0:T(8,128)(2,1)}, u32[]{:S(2)}) copy-start(bf16[2048,128]{1,0:T(8,128)(2,1)} %get-tuple-element.5) | copy-start | bytes 1572868

commit v7 on v6

--- a/solution.py
+++ b/solution.py
@@ -63,15 +63,13 @@
     lane = lax.broadcasted_iota(jnp.int32, (32, 512), 1) % 64
     narrow = weight_ref[...].astype(F32)
     weight = jnp.concatenate([jnp.broadcast_to(narrow[h : h + 1], (64, 128)) for h in range(8)], axis=0).astype(BF16)
-
-    def step(k, total):
-        rows = pair_ref[pl.ds(k * 8, 8)].reshape(256, 128).astype(F32)
+    total = jnp.zeros((32, 512), F32)
+    for k in range(8):
+        rows = pair_ref[k * 8 : k * 8 + 8].reshape(256, 128).astype(F32)
         spread = dot_nt(layer_norm(rows).astype(BF16), weight)
         for one in range(8):
             total = jnp.where(lane == k * 8 + one, spread[one * 32 : one * 32 + 32], total)
-        return total
-
-    total = lax.fori_loop(0, 8, step, jnp.zeros((32, 512), F32)).astype(BF16)
+    total = total.astype(BF16)
     for t in range(4):
         out_ref[t] = total[:, t * 128 : t * 128 + 128]
 
@@ -95,6 +93,7 @@
     bias = jnp.concatenate(
         [bias_ref[t, dx, 2 * e : 2 * e + 2].reshape(512, 128) for e in range(2) for t in range(4)], axis=1
     ).astype(F32)
+    gated, cells = [], []
     for n in range(2):
         wide = jnp.concatenate([jnp.concatenate([qd[n, sp * 2 + e]] * 4, axis=1) * mask[...] for e in range(2)], axis=1)
         score = dot(kk[n], wide) + bias
@@ -115,11 +114,13 @@
                     parts.append(part)
             halves.append(parts)
         ot = jnp.concatenate([jnp.where(low, a, b) for a, b in zip(*halves)], axis=0)
-        gated = (gt[n, sp].astype(F32) * ot).astype(BF16)
-        x = x_ref[pl.ds(sp * 4, 4), n].reshape(128, C).astype(F32)
-        new = x + dot_tn(gated, wo[...])
+        gated.append((gt[n, sp].astype(F32) * ot).astype(BF16))
+        cells.append(x_ref[pl.ds(sp * 4, 4), n].reshape(128, C).astype(F32))
+    new = jnp.concatenate(cells, axis=0) + dot_tn(jnp.concatenate(gated, axis=1), wo[...])
+    for n in range(2):
         for ch in range(2):
-            mid[n, ch] = new[:, ch * 128 : ch * 128 + 128]
+            mid[n, ch] = new[n * 128 : n * 128 + 128, ch * 128 : ch * 128 + 128]
+    for n in range(2):
         for ch in range(2):
             for a in range(4):
                 mix[pl.ds(sp * 512 + n * 8 + ch * 4 + a, 32, stride=16), :] = mid[n, ch, pl.ds(a, 32, stride=4), :]
@@ -425,7 +426,7 @@
             lax.fori_loop(0, 16, scatter, 0, unroll=True)
         return carry
 
-    lax.fori_loop(0, 4, attend, 0)
+    lax.fori_loop(0, 4, attend, 0, unroll=True)
     cells[here] = sendbuf[here]
     for copy in copies:
         copy.wait_send()

time: 75.8 us -> 74.4 us (0.982)
  Pallas kernels: 72.1 us -> 70.7 us
    pallas_call x1, Pallas kernels: 72.1 us -> 70.7 us  [body(): pl.pallas_call(whole_kernel, out_shape=(jax.ShapeDtypeStruct((256, 4, C),...]
where the time goes in v7:
time: 74.4 us; the launch traced here: 74.2 us
  Pallas kernels  70.7 us (95%)
  local copies, waits for them, and re-layouts  2.87 us (4%)
    pallas_call x1, Pallas kernels, body(): pl.pallas_call(whole_kernel, out_shape=(jax.ShapeDtypeStruct((256, 4, C),...  70.7 us
    unnamed x4, local copies, waits for them, and re-layouts  2.87 us

profile of v7, /device:TPU:1, one launch (start us, length us, event | category | flops | bytes accessed | tf_op | source)
XLA Modules:
  0.0 74.2 jit_solution(12331282888470911705)
XLA Ops:
  0.6 70.7 %evoformer.1 = (bf16[256,4,256]{2,1,0:T(4,128)(2,1)}, bf16[2048,128]{1,0:T(8,128)(2,1)}) custom-call(bf16[16,2,32,256]{3,2,1,0:T(8,128)(2,1)} %bitcast.4, bf16[64,32,128]{2,1,0:T(8,128)(2,1)} %pair_hbm.1, bf16[8,128]{1,0:T(8,128)(2,1)} %bitcast.7, bf16[256,1024]{1,0:T(8,128)(2,1)} %rw_hbm.1, bf16[256,256]{1,0:T(8,128)(2,1)} %ro_hbm.1, ...), custom_call_target="tpu_custom_call" | custom-call | tf_op jit(solution)/shard_map/evoformer/pallas_call | solution.py:552
  71.4 0.0 copy-start
  71.4 2.1 %copy.15 = bf16[256,4,256]{2,1,0:T(4,128)(2,1)} copy(bf16[256,4,256]{2,1,0:T(4,128)(2,1)} %get-tuple-element.8) | data formatting | bytes 1048576
  73.4 0.0 copy-done
  73.5 0.8 %copy.16 = bf16[64,32,128]{2,1,0:T(8,128)(2,1)} copy(bf16[64,32,128]{2,1,0:T(8,128)(2,1)S(1)} %bitcast.5) | data formatting | bytes 1048576
Async XLA Ops:
  71.4 2.1 %copy-start = (bf16[2048,128]{1,0:T(8,128)(2,1)S(1)}, bf16[2048,128]{1,0:T(8,128)(2,1)}, u32[]{:S(2)}) copy-start(bf16[2048,128]{1,0:T(8,128)(2,1)} %get-tuple-element.5) | copy-start | bytes 1572868

commit v8 on v7

--- a/solution.py
+++ b/solution.py
@@ -262,8 +262,7 @@
     need("bw")
     pair_bias(pair, bw, own)
     mine_at = bias.at[:, 0, pos["y"], pos["z"], core]
-    place = pltpu.make_async_copy(own, mine_at, lsem.at[0])
-    place.start()
+    bias[:, 0, pos["y"], pos["z"], core] = own[...]
     pl.semaphore_wait(barrier, 21)
 
     def scatter_x(k, carry):
@@ -336,7 +335,6 @@
     copies.extend(t_x)
     lax.fori_loop(1, 16, scatter_x, 0)
 
-    place.wait()
     arrived(low_z)
     mine = bias.at[LOW, 0, py, :, core]
     low_y = three("y", mine, mine, 9)

time: 74.4 us -> 74.4 us (level)
  no operation moved by 1% of the time
where the time goes in v8:
time: 74.4 us; the launch traced here: 74.3 us
  Pallas kernels  70.8 us (95%)
  local copies, waits for them, and re-layouts  2.87 us (4%)
    pallas_call x1, Pallas kernels, body(): pl.pallas_call(whole_kernel, out_shape=(jax.ShapeDtypeStruct((256, 4, C),...  70.8 us
    unnamed x4, local copies, waits for them, and re-layouts  2.87 us

profile of v8, /device:TPU:1, one launch (start us, length us, event | category | flops | bytes accessed | tf_op | source)
XLA Modules:
  0.0 74.3 jit_solution(11440086497570845589)
XLA Ops:
  0.6 70.8 %evoformer.1 = (bf16[256,4,256]{2,1,0:T(4,128)(2,1)}, bf16[2048,128]{1,0:T(8,128)(2,1)}) custom-call(bf16[16,2,32,256]{3,2,1,0:T(8,128)(2,1)} %bitcast.4, bf16[64,32,128]{2,1,0:T(8,128)(2,1)} %pair_hbm.1, bf16[8,128]{1,0:T(8,128)(2,1)} %bitcast.7, bf16[256,1024]{1,0:T(8,128)(2,1)} %rw_hbm.1, bf16[256,256]{1,0:T(8,128)(2,1)} %ro_hbm.1, ...), custom_call_target="tpu_custom_call" | custom-call | tf_op jit(solution)/shard_map/evoformer/pallas_call | solution.py:550
  71.4 0.0 copy-start
  71.4 2.1 %copy.15 = bf16[256,4,256]{2,1,0:T(4,128)(2,1)} copy(bf16[256,4,256]{2,1,0:T(4,128)(2,1)} %get-tuple-element.8) | data formatting | bytes 1048576
  73.5 0.0 copy-done
  73.5 0.8 %copy.16 = bf16[64,32,128]{2,1,0:T(8,128)(2,1)} copy(bf16[64,32,128]{2,1,0:T(8,128)(2,1)S(1)} %bitcast.5) | data formatting | bytes 1048576
Async XLA Ops:
  71.4 2.1 %copy-start = (bf16[2048,128]{1,0:T(8,128)(2,1)S(1)}, bf16[2048,128]{1,0:T(8,128)(2,1)}, u32[]{:S(2)}) copy-start(bf16[2048,128]{1,0:T(8,128)(2,1)} %get-tuple-element.5) | copy-start | bytes 1572868
